TPU v7x, 32 devices: a whole 2x2x4 slice. The times are simulated.
32 devices in a mesh: dp: 8 (over z, x), pipe: 4 (over y, core).
Axes of the slice: x: 2, y: 2, z: 4, core: 2. Of those that a mesh axis runs over, the one named last changes fastest.
Arguments:
- patch_states: bfloat16 [16, 256, 1024], P('dp'), may hold values from -6 to 6
- byte_states: bfloat16 [16, 640, 1024], P('dp'), may hold values from -6 to 6
- cotangent: bfloat16 [16, 256, 1024], P('dp'), may hold values from -6 to 6
- patch_lengths: int32 [16, 256], P('dp'), may hold values from 1 to 8, 640 in all within a row
- row_lengths: int32 [16], P('dp'), may hold values from 1 to 256, 2560 in all
- attn_weights: bfloat16 [2, 3, 1024, 1024], P(None, None, ('dp', 'pipe')), may hold values from -0.1875 to 0.1875
- out_weights: bfloat16 [2, 1024, 1024], P(None, ('dp', 'pipe')), may hold values from -0.5 to 0.5
- gate_up: bfloat16 [2, 1024, 2816], P(None, ('dp', 'pipe')), may hold values from -0.1875 to 0.1875
- down_weight: bfloat16 [2816, 1024], P(('dp', 'pipe')), may hold values from -0.109375 to 0.109375
- gains: float32 [4, 1024], replicated, may hold values from 0.1 to 1.9
Outputs:
- outputs: bfloat16 [16, 256, 1024], P('dp', 'pipe')
- grad_patches: bfloat16 [16, 256, 1024], P('dp', 'pipe')
- grad_bytes: bfloat16 [16, 640, 1024], P('dp', 'pipe')
- grad_attn: float32 [2, 3, 1024, 1024], P(None, None, ('dp', 'pipe'))
- grad_out: float32 [2, 1024, 1024], P(None, ('dp', 'pipe'))
- grad_gate_up: float32 [2, 1024, 2816], P(None, ('dp', 'pipe'))
- grad_down: float32 [2816, 1024], P(('dp', 'pipe'))
- grad_gains: float32 [4, 1024], P(None, ('dp', 'pipe'))
Inputs may be any that keep to these rules, and one draw needn't show every extreme that they name: `patch_lengths`: each row's 256 entries sum to 640; every row has a patch of exactly 8 bytes. Patches at or after row_lengths[r] are padding and are no keys of the global attention; some row is full.
All inputs are finite; a program needn't handle non-finite values. No bound on the sum of `row_lengths` on one device may be relied on, other than what follows from the above.
Results may differ from a plain program's by a relative error of at most 0.028.
Values may be sent and summed in bfloat16 or wider, within the bound.
A program may use at most 512 MiB of HBM per device.

v0:
```python
import jax
import jax.numpy as jnp
from jax import lax
from jax.sharding import PartitionSpec as P

HEADS = 16
HEAD_DIM = 64
PATCH_MAX = 8


EPSILON = 1e-06
NEGATIVE = -1e30


def as_sent(x):
    return jax.tree.map(lambda a: a.astype(jnp.bfloat16) if a.dtype == jnp.float32 else a, x)


def shifted(block, axis, distance):
    devices = range(lax.axis_size(axis))
    route = [(i - distance, i) for i in devices if i - distance in devices]
    return lax.ppermute(block, axis, route)


def product(left, right):
    return jnp.dot(left, right, preferred_element_type=jnp.float32)


def product_left(left, right):
    return lax.dot_general(
        left, right, (((0,), (0,)), ((), ())), preferred_element_type=jnp.float32
    )


def product_right(left, right):
    return lax.dot_general(
        left, right, (((1,), (1,)), ((), ())), preferred_element_type=jnp.float32
    )


def pad_columns(values, width):
    return jnp.pad(values, ((0, 0), (0, width - values.shape[1])))


def columns_of(block, first, count):
    return block[:, first : first + count]


def norm_rows(values, gain):
    factor = lax.rsqrt(jnp.mean(values * values, axis=-1, keepdims=True) + EPSILON)
    return (values * factor * gain, factor)


def norm_back(values, factor, gain, gradient):
    weighted = gradient * gain
    grad_gain = jnp.sum(gradient * values * factor, axis=0)
    grad_values = factor * weighted - values * factor**3 * jnp.mean(
        weighted * values, axis=-1, keepdims=True
    )
    return (grad_values, grad_gain)


def split_heads(values):
    return values.reshape(values.shape[0], HEADS, HEAD_DIM)


def pick_row(source, micro_id):
    return lax.dynamic_index_in_dim(source, micro_id, 0, keepdims=False)


def place_row(target, new_row, micro_id, active):
    merged = jnp.where(active, new_row, pick_row(target, micro_id))
    return lax.dynamic_update_index_in_dim(target, merged, micro_id, 0)


def cross_state(patch_row, byte_row, patch_sizes, attn_stack, out_stack, gain_rows):
    patch_f = patch_row.astype(jnp.float32)
    byte_f = byte_row.astype(jnp.float32)
    normed_q, factor_q = norm_rows(patch_f, gain_rows[0])
    normed_b, factor_b = norm_rows(byte_f, gain_rows[1])
    normed_q = normed_q.astype(jnp.bfloat16)
    normed_b = normed_b.astype(jnp.bfloat16)
    row_count = patch_f.shape[0]
    byte_count = byte_f.shape[0]
    queries = split_heads(product(normed_q, attn_stack[0, 0]).astype(jnp.bfloat16))
    key_rows = product(normed_b, attn_stack[0, 1]).astype(jnp.bfloat16)
    value_rows = product(normed_b, attn_stack[0, 2]).astype(jnp.bfloat16)
    starts = (jnp.cumsum(patch_sizes) - patch_sizes).astype(jnp.int32)
    offsets = jnp.arange(PATCH_MAX, dtype=jnp.int32)
    byte_index = jnp.minimum(starts[:, None] + offsets[None, :], byte_count - 1).astype(jnp.int32)
    live_slot = offsets[None, :] < patch_sizes[:, None]
    key_win = key_rows[byte_index].reshape(row_count, PATCH_MAX, HEADS, HEAD_DIM)
    value_win = value_rows[byte_index].reshape(row_count, PATCH_MAX, HEADS, HEAD_DIM)
    scores = jnp.einsum(
        "phe,plhe->phl", queries, key_win, preferred_element_type=jnp.float32
    ) * HEAD_DIM ** (-0.5)
    attention = jax.nn.softmax(jnp.where(live_slot[:, None, :], scores, NEGATIVE), axis=-1)
    attention_low = attention.astype(jnp.bfloat16)
    mixed_rows = jnp.einsum(
        "phl,plhe->phe", attention_low, value_win, preferred_element_type=jnp.float32
    )
    mixed_rows = mixed_rows.reshape(row_count, -1).astype(jnp.bfloat16)
    residual_out = (patch_f + product(mixed_rows, out_stack[0])).astype(jnp.bfloat16)
    saved_state = (
        patch_f,
        byte_f,
        normed_q,
        factor_q,
        normed_b,
        factor_b,
        queries,
        key_win,
        value_win,
        byte_index,
        attention,
        attention_low,
        mixed_rows,
    )
    return (residual_out, saved_state)


def cross_back(patch_row, byte_row, patch_sizes, attn_stack, out_stack, gain_rows, grad_residual):
    residual_out, saved_state = cross_state(
        patch_row, byte_row, patch_sizes, attn_stack, out_stack, gain_rows
    )
    (
        patch_f,
        byte_f,
        normed_q,
        factor_q,
        normed_b,
        factor_b,
        queries,
        key_win,
        value_win,
        byte_index,
        attention,
        attention_low,
        mixed_rows,
    ) = saved_state
    score_scale = HEAD_DIM ** (-0.5)
    row_count = patch_f.shape[0]
    byte_count = byte_f.shape[0]
    feature = patch_f.shape[1]
    grad_out = product_left(mixed_rows, grad_residual)
    grad_mixed = split_heads(product_right(grad_residual, out_stack[0]).astype(jnp.bfloat16))
    grad_attention = jnp.einsum(
        "phe,plhe->phl", grad_mixed, value_win, preferred_element_type=jnp.float32
    )
    grad_value_win = jnp.einsum(
        "phl,phe->plhe", attention_low, grad_mixed, preferred_element_type=jnp.float32
    )
    grad_scores = attention * (
        grad_attention - jnp.sum(attention * grad_attention, axis=-1, keepdims=True)
    )
    grad_scores = grad_scores.astype(jnp.bfloat16)
    grad_queries = (
        jnp.einsum("phl,plhe->phe", grad_scores, key_win, preferred_element_type=jnp.float32)
        * score_scale
    )
    grad_queries = grad_queries.reshape(row_count, -1).astype(jnp.bfloat16)
    grad_key_win = (
        jnp.einsum("phl,phe->plhe", grad_scores, queries, preferred_element_type=jnp.float32)
        * score_scale
    )
    flat_index = byte_index.reshape(-1)
    empty_bytes = jnp.zeros((byte_count, feature), jnp.float32)
    grad_keys = (
        empty_bytes.at[flat_index].add(grad_key_win.reshape(-1, feature)).astype(jnp.bfloat16)
    )
    grad_values = (
        empty_bytes.at[flat_index].add(grad_value_win.reshape(-1, feature)).astype(jnp.bfloat16)
    )
    grad_proj = (
        product_left(normed_q, grad_queries),
        product_left(normed_b, grad_keys),
        product_left(normed_b, grad_values),
    )
    grad_normed_q = product_right(grad_queries, attn_stack[0, 0])
    grad_normed_b = product_right(grad_keys, attn_stack[0, 1]) + product_right(
        grad_values, attn_stack[0, 2]
    )
    grad_patch, gain_query = norm_back(patch_f, factor_q, gain_rows[0], grad_normed_q)
    grad_byte, gain_bytes = norm_back(byte_f, factor_b, gain_rows[1], grad_normed_b)
    grad_patch = (grad_patch + grad_residual.astype(jnp.float32)).astype(jnp.bfloat16)
    return (grad_proj, grad_out, gain_query, gain_bytes, grad_patch, grad_byte.astype(jnp.bfloat16))


def attention_block(queries, key_rows, begin_row, seq_length):
    scores = jnp.einsum(
        "qhe,khe->hqk", queries, key_rows, preferred_element_type=jnp.float32
    ) * HEAD_DIM ** (-0.5)
    query_pos = begin_row + jnp.arange(queries.shape[0], dtype=jnp.int32)
    key_pos = jnp.arange(key_rows.shape[0], dtype=jnp.int32)
    allowed = (key_pos[None, :] <= query_pos[:, None]) & (key_pos[None, :] < seq_length)
    return jax.nn.softmax(jnp.where(allowed[None], scores, NEGATIVE), axis=-1)


def global_state(residual_in, seq_length, attn_stack, gain_rows):
    residual_f = residual_in.astype(jnp.float32)
    normed, factor = norm_rows(residual_f, gain_rows[2])
    normed = normed.astype(jnp.bfloat16)
    queries = split_heads(product(normed, attn_stack[1, 0]).astype(jnp.bfloat16))
    key_rows = split_heads(product(normed, attn_stack[1, 1]).astype(jnp.bfloat16))
    value_rows = split_heads(product(normed, attn_stack[1, 2]).astype(jnp.bfloat16))
    row_count = queries.shape[0]
    block_rows = min(512, row_count)
    pieces = []
    for begin_row in range(0, row_count, block_rows):
        end_row = begin_row + block_rows
        attention = attention_block(
            queries[begin_row:end_row], key_rows[:end_row], begin_row, seq_length
        )
        pieces.append(
            jnp.einsum(
                "hqk,khe->qhe",
                attention.astype(jnp.bfloat16),
                value_rows[:end_row],
                preferred_element_type=jnp.float32,
            )
        )
    mixed_rows = jnp.concatenate(pieces, axis=0).reshape(row_count, -1).astype(jnp.bfloat16)
    return (residual_f, normed, factor, queries, key_rows, value_rows, mixed_rows)


def global_back(residual_in, seq_length, attn_stack, out_stack, gain_rows, grad_residual):
    residual_f, normed, factor, queries, key_rows, value_rows, mixed_rows = global_state(
        residual_in, seq_length, attn_stack, gain_rows
    )
    score_scale = HEAD_DIM ** (-0.5)
    row_count = queries.shape[0]
    block_rows = min(512, row_count)
    grad_out = product_left(mixed_rows, grad_residual)
    grad_mixed = split_heads(product_right(grad_residual, out_stack[1]).astype(jnp.bfloat16))
    grad_keys = jnp.zeros(key_rows.shape, jnp.float32)
    grad_values = jnp.zeros(value_rows.shape, jnp.float32)
    pieces = []
    for begin_row in range(0, row_count, block_rows):
        end_row = begin_row + block_rows
        block_q = queries[begin_row:end_row]
        attention = attention_block(block_q, key_rows[:end_row], begin_row, seq_length)
        attention_low = attention.astype(jnp.bfloat16)
        grad_piece = grad_mixed[begin_row:end_row]
        grad_attention = jnp.einsum(
            "qhe,khe->hqk", grad_piece, value_rows[:end_row], preferred_element_type=jnp.float32
        )
        grad_scores = attention * (
            grad_attention - jnp.sum(attention * grad_attention, axis=-1, keepdims=True)
        )
        grad_scores = grad_scores.astype(jnp.bfloat16)
        pieces.append(
            jnp.einsum(
                "hqk,khe->qhe", grad_scores, key_rows[:end_row], preferred_element_type=jnp.float32
            )
            * score_scale
        )
        grad_keys = grad_keys.at[:end_row].add(
            jnp.einsum("hqk,qhe->khe", grad_scores, block_q, preferred_element_type=jnp.float32)
            * score_scale
        )
        grad_values = grad_values.at[:end_row].add(
            jnp.einsum(
                "hqk,qhe->khe", attention_low, grad_piece, preferred_element_type=jnp.float32
            )
        )
    grad_queries = jnp.concatenate(pieces, axis=0).reshape(row_count, -1).astype(jnp.bfloat16)
    grad_keys = grad_keys.reshape(row_count, -1).astype(jnp.bfloat16)
    grad_values = grad_values.reshape(row_count, -1).astype(jnp.bfloat16)
    grad_proj = (
        product_left(normed, grad_queries),
        product_left(normed, grad_keys),
        product_left(normed, grad_values),
    )
    grad_normed = (
        product_right(grad_queries, attn_stack[1, 0])
        + product_right(grad_keys, attn_stack[1, 1])
        + product_right(grad_values, attn_stack[1, 2])
    )
    grad_input, grad_gain = norm_back(residual_f, factor, gain_rows[2], grad_normed)
    grad_input = (grad_input + grad_residual.astype(jnp.float32)).astype(jnp.bfloat16)
    return (grad_proj, grad_out, grad_gain, grad_input)


def gate_state(residual_in, gate_stack, gain_rows):
    residual_f = residual_in.astype(jnp.float32)
    normed, factor = norm_rows(residual_f, gain_rows[3])
    normed = normed.astype(jnp.bfloat16)
    gate_rows = product(normed, gate_stack[0])
    up_rows = product(normed, gate_stack[1])
    hidden = (jax.nn.silu(gate_rows) * up_rows).astype(jnp.bfloat16)
    return (residual_f, normed, factor, gate_rows, up_rows, hidden)


def gate_back(residual_in, gate_stack, gain_rows, grad_residual, grad_hidden):
    residual_f, normed, factor, gate_rows, up_rows, hidden = gate_state(
        residual_in, gate_stack, gain_rows
    )
    sigmoid_gate = jax.nn.sigmoid(gate_rows)
    grad_hidden_f = grad_hidden.astype(jnp.float32)
    grad_gate = grad_hidden_f * up_rows * sigmoid_gate * (1.0 + gate_rows * (1.0 - sigmoid_gate))
    grad_gate = grad_gate.astype(jnp.bfloat16)
    grad_up = (grad_hidden_f * gate_rows * sigmoid_gate).astype(jnp.bfloat16)
    grad_proj = (product_left(normed, grad_gate), product_left(normed, grad_up))
    grad_normed = product_right(grad_gate, gate_stack[0]) + product_right(grad_up, gate_stack[1])
    grad_input, grad_gain = norm_back(residual_f, factor, gain_rows[3], grad_normed)
    grad_input = (grad_input + grad_residual.astype(jnp.float32)).astype(jnp.bfloat16)
    return (grad_proj, grad_gain, grad_input)


def local(
    patch_states,
    byte_states,
    cotangent,
    patch_lengths,
    row_lengths,
    attn_weights,
    out_weights,
    gate_up,
    down_weight,
    gains,
):
    feature = attn_weights.shape[3]
    hidden_width = gate_up.shape[2]
    pack_width = max(4 * feature, 2 * hidden_width)
    grad_width = pack_width + 2
    attn_stack, out_stack, gate_stack, down_rows = (
        lax.all_gather(attn_weights, ("dp", "pipe"), axis=2, tiled=True),
        lax.all_gather(out_weights, ("dp", "pipe"), axis=1, tiled=True),
        lax.all_gather(gate_up, ("dp", "pipe"), axis=1, tiled=True),
        lax.all_gather(down_weight, ("dp", "pipe"), axis=0, tiled=True),
    )
    section_id = lax.axis_index("pipe")
    last_section = 3
    micro_count = patch_states.shape[0]
    row_count = patch_states.shape[1]
    byte_count = byte_states.shape[1]
    zero_residual = jnp.zeros((row_count, feature), jnp.bfloat16)
    zero_hidden = jnp.zeros((row_count, hidden_width), jnp.bfloat16)
    zero_bytes = jnp.zeros((byte_count, feature), jnp.bfloat16)
    zero_gain = jnp.zeros((feature,), jnp.float32)
    zero_pack = jnp.zeros((feature, grad_width), jnp.float32)

    def pack_grads(matrices, gain_first, gain_second):
        main = pad_columns(jnp.concatenate(matrices, axis=1), pack_width)
        return jnp.concatenate([main, gain_first[:, None], gain_second[:, None]], axis=1)

    def forward_cross(operand):
        patch_row, byte_row, patch_sizes, seq_length, residual_in, hidden_in = operand
        residual_out, saved_state = cross_state(
            patch_row, byte_row, patch_sizes, attn_stack, out_stack, gains
        )
        return (residual_out, zero_hidden)

    def forward_global(operand):
        patch_row, byte_row, patch_sizes, seq_length, residual_in, hidden_in = operand
        saved_state = global_state(residual_in, seq_length, attn_stack, gains)
        residual_out = (saved_state[0] + product(saved_state[6], out_stack[1])).astype(jnp.bfloat16)
        return (residual_out, zero_hidden)

    def forward_gate(operand):
        patch_row, byte_row, patch_sizes, seq_length, residual_in, hidden_in = operand
        return (residual_in, gate_state(residual_in, gate_stack, gains)[5])

    def forward_down(operand):
        patch_row, byte_row, patch_sizes, seq_length, residual_in, hidden_in = operand
        result = (residual_in.astype(jnp.float32) + product(hidden_in, down_rows)).astype(
            jnp.bfloat16
        )
        return (result, zero_hidden)

    def forward_none(operand):
        return (zero_residual, zero_hidden)

    ticks = micro_count + last_section
    stash_residual = jnp.zeros((micro_count, row_count, feature), jnp.bfloat16)
    stash_hidden = jnp.zeros((micro_count, row_count, hidden_width), jnp.bfloat16)
    result_rows = jnp.zeros_like(patch_states)
    arriving = (zero_residual, zero_hidden)
    for tick in range(ticks):
        offset = tick - section_id
        active = (offset >= 0) & (offset < micro_count)
        micro_id = jnp.clip(offset, 0, micro_count - 1)
        stash_residual = place_row(stash_residual, arriving[0], micro_id, active)
        stash_hidden = place_row(stash_hidden, arriving[1], micro_id, active)
        operand = (
            pick_row(patch_states, micro_id),
            pick_row(byte_states, micro_id),
            pick_row(patch_lengths, micro_id),
            pick_row(row_lengths, micro_id),
            arriving[0],
            arriving[1],
        )
        leaving = lax.switch(
            jnp.where(active, section_id, 4),
            [forward_cross, forward_global, forward_gate, forward_down, forward_none],
            operand,
        )
        result_rows = place_row(
            result_rows, leaving[0], micro_id, active & (section_id == last_section)
        )
        arriving = shifted((as_sent(leaving[0]), as_sent(leaving[1])), "pipe", 1)

    def backward_cross(operand):
        (
            patch_row,
            byte_row,
            patch_sizes,
            seq_length,
            residual_in,
            hidden_in,
            grad_residual,
            grad_hidden,
            cot_row,
        ) = operand
        grad_proj, grad_out, gain_query, gain_bytes, grad_patch, grad_byte = cross_back(
            patch_row, byte_row, patch_sizes, attn_stack, out_stack, gains, grad_residual
        )
        contribution = pack_grads(
            [grad_proj[0], grad_proj[1], grad_proj[2], grad_out], gain_query, gain_bytes
        )
        return (contribution, zero_residual, zero_hidden, grad_patch, grad_byte)

    def backward_global(operand):
        (
            patch_row,
            byte_row,
            patch_sizes,
            seq_length,
            residual_in,
            hidden_in,
            grad_residual,
            grad_hidden,
            cot_row,
        ) = operand
        grad_proj, grad_out, grad_gain, grad_input = global_back(
            residual_in, seq_length, attn_stack, out_stack, gains, grad_residual
        )
        contribution = pack_grads(
            [grad_proj[0], grad_proj[1], grad_proj[2], grad_out], grad_gain, zero_gain
        )
        return (contribution, grad_input, zero_hidden, zero_residual, zero_bytes)

    def backward_gate(operand):
        (
            patch_row,
            byte_row,
            patch_sizes,
            seq_length,
            residual_in,
            hidden_in,
            grad_residual,
            grad_hidden,
            cot_row,
        ) = operand
        grad_proj, grad_gain, grad_input = gate_back(
            residual_in, gate_stack, gains, grad_residual, grad_hidden
        )
        contribution = pack_grads([grad_proj[0], grad_proj[1]], grad_gain, zero_gain)
        return (contribution, grad_input, zero_hidden, zero_residual, zero_bytes)

    def backward_down(operand):
        (
            patch_row,
            byte_row,
            patch_sizes,
            seq_length,
            residual_in,
            hidden_in,
            grad_residual,
            grad_hidden,
            cot_row,
        ) = operand
        contribution = pad_columns(
            product_left(hidden_in, cot_row).reshape(feature, hidden_width), grad_width
        )
        grad_hidden_out = product_right(cot_row, down_rows).astype(jnp.bfloat16)
        return (contribution, cot_row, grad_hidden_out, zero_residual, zero_bytes)

    def backward_none(operand):
        return (zero_pack, zero_residual, zero_hidden, zero_residual, zero_bytes)

    grad_pack = zero_pack
    returning = (zero_residual, zero_hidden)
    grad_patches = jnp.zeros_like(patch_states)
    grad_bytes = jnp.zeros_like(byte_states)
    for tick in range(ticks):
        offset = tick - (last_section - section_id)
        active = (offset >= 0) & (offset < micro_count)
        micro_id = jnp.clip(offset, 0, micro_count - 1)
        operand = (
            pick_row(patch_states, micro_id),
            pick_row(byte_states, micro_id),
            pick_row(patch_lengths, micro_id),
            pick_row(row_lengths, micro_id),
            pick_row(stash_residual, micro_id),
            pick_row(stash_hidden, micro_id),
            returning[0],
            returning[1],
            pick_row(cotangent, micro_id),
        )
        contribution, grad_residual, grad_hidden, grad_patch, grad_byte = lax.switch(
            jnp.where(active, section_id, 4),
            [backward_cross, backward_global, backward_gate, backward_down, backward_none],
            operand,
        )
        grad_pack = grad_pack + contribution
        first_section = active & (section_id == 0)
        grad_patches = place_row(grad_patches, grad_patch, micro_id, first_section)
        grad_bytes = place_row(grad_bytes, grad_byte, micro_id, first_section)
        returning = (
            shifted(as_sent(grad_residual), "pipe", -1).astype(grad_residual.dtype),
            shifted(as_sent(grad_hidden), "pipe", -1).astype(grad_hidden.dtype),
        )
    shares = (
        lax.psum_scatter(
            result_rows.astype(jnp.float32).astype(jnp.bfloat16),
            "pipe",
            scatter_dimension=1,
            tiled=True,
        ).astype(jnp.float32),
        lax.psum_scatter(
            grad_patches.astype(jnp.float32).astype(jnp.bfloat16),
            "pipe",
            scatter_dimension=1,
            tiled=True,
        ).astype(jnp.float32),
        lax.psum_scatter(
            grad_bytes.astype(jnp.float32).astype(jnp.bfloat16),
            "pipe",
            scatter_dimension=1,
            tiled=True,
        ).astype(jnp.float32),
    )
    masked = [jnp.where(section_id == section, grad_pack, 0.0) for section in range(4)]
    cross_part = masked[0]
    global_part = masked[1]
    gate_part = masked[2]
    summed = (
        lax.psum_scatter(
            jnp.stack(
                [
                    jnp.stack(
                        [
                            columns_of(cross_part, 0, feature),
                            columns_of(cross_part, feature, feature),
                            columns_of(cross_part, 2 * feature, feature),
                        ]
                    ),
                    jnp.stack(
                        [
                            columns_of(global_part, 0, feature),
                            columns_of(global_part, feature, feature),
                            columns_of(global_part, 2 * feature, feature),
                        ]
                    ),
                ]
            ),
            ("dp", "pipe"),
            scatter_dimension=2,
            tiled=True,
        ),
        lax.psum_scatter(
            jnp.stack(
                [
                    columns_of(cross_part, 3 * feature, feature),
                    columns_of(global_part, 3 * feature, feature),
                ]
            ),
            ("dp", "pipe"),
            scatter_dimension=1,
            tiled=True,
        ),
        lax.psum_scatter(
            jnp.stack(
                [
                    columns_of(gate_part, 0, hidden_width),
                    columns_of(gate_part, hidden_width, hidden_width),
                ]
            ),
            ("dp", "pipe"),
            scatter_dimension=1,
            tiled=True,
        ),
        lax.psum_scatter(
            columns_of(masked[3], 0, hidden_width).reshape(-1, feature),
            ("dp", "pipe"),
            scatter_dimension=0,
            tiled=True,
        ),
        lax.psum_scatter(
            jnp.stack(
                [
                    cross_part[:, pack_width],
                    cross_part[:, pack_width + 1],
                    global_part[:, pack_width],
                    gate_part[:, pack_width],
                ]
            ),
            ("dp", "pipe"),
            scatter_dimension=1,
            tiled=True,
        ),
    )
    return (
        shares[0].astype(jnp.bfloat16),
        shares[1].astype(jnp.bfloat16),
        shares[2].astype(jnp.bfloat16),
        summed[0],
        summed[1],
        summed[2],
        summed[3],
        summed[4],
    )


def solution(mesh):
    placed = (
        P("dp", None, None),
        P("dp", None, None),
        P("dp", None, None),
        P("dp", None),
        P("dp"),
        P(None, None, ("dp", "pipe"), None),
        P(None, ("dp", "pipe"), None),
        P(None, ("dp", "pipe"), None),
        P(("dp", "pipe"), None),
        P(),
    )
    return jax.shard_map(
        local,
        mesh=mesh,
        in_specs=placed,
        out_specs=(
            P("dp", "pipe", None),
            P("dp", "pipe", None),
            P("dp", "pipe", None),
            P(None, None, ("dp", "pipe"), None),
            P(None, ("dp", "pipe"), None),
            P(None, ("dp", "pipe"), None),
            P(("dp", "pipe"), None),
            P(None, ("dp", "pipe")),
        ),
        check_vma=False,
    )
```

profile of v0, /device:TPU:0, one launch (start us, length us, event | category | flops | bytes accessed | tf_op | source)
XLA Modules:
  0.0 2693.2 jit_solution(6084419606835341572)
XLA Ops:
  10.0 95.1 %all-gather.9.cloned.1.call-done = bf16[2,1024,2816]{2,1,0:T(8,128)(2,1)} async-done(((bf16[2,32,2816]{2,1,0:T(8,128)(2,1)}), bf16[2,1024,2816]{2,1,0:T(8,128)(2,1)}) %all-gather.9.cloned.1.call-update) | async-done | bytes 11534352 | tf_op jit(solution)/shard_map/all_gather | solution.py:329
  105.1 63.3 %all-gather.7.cloned.1.call-done = bf16[2,1024,1024]{2,1,0:T(8,128)(2,1)} async-done(((bf16[2,32,1024]{2,1,0:T(8,128)(2,1)}), bf16[2,1024,1024]{2,1,0:T(8,128)(2,1)}) %all-gather.7.cloned.1.call-update) | async-done | bytes 4194320 | tf_op jit(solution)/shard_map/all_gather | solution.py:328
  168.5 97.3 %all-gather.5.cloned.1.call-done = bf16[2,3,1024,1024]{3,2,1,0:T(8,128)(2,1)} async-done(((bf16[2,3,32,1024]{3,2,1,0:T(8,128)(2,1)}), bf16[2,3,1024,1024]{3,2,1,0:T(8,128)(2,1)}) %all-gather.5.cloned.1.call-update) | async-done | bytes 12582928 | tf_op jit(solution)/shard_map/all_gather | solution.py:327
  265.8 68.4 %all-gather.11.cloned.1.call-done = bf16[2816,1024]{1,0:T(8,128)(2,1)} async-done(((bf16[88,1024]{1,0:T(8,128)(2,1)}), bf16[2816,1024]{1,0:T(8,128)(2,1)}) %all-gather.11.cloned.1.call-update) | async-done | bytes 5767184 | tf_op jit(solution)/shard_map/all_gather | solution.py:330
  334.1 88.2 %conditional.10 = (bf16[256,1024]{1,0:T(8,128)(2,1)}, bf16[256,2816]{1,0:T(8,128)(2,1)}) conditional(s32[]{:T(128)} %clamp.30, (bf16[2,256,1024]{2,1,0:T(8,128)(2,1)}, s32[]{:T(128)}, s32[2,256]{1,0:T(2,128)}, f32[4,1024]{1,0:T(4,128)}, bf16[2,3,1024,1024]{3,2,1,0:T(8,128)(2,1)}, ...), branch_computations={%region_0.7_spmd, %region_7.10_spmd, %region_10.11_spmd, %region_1... | conditional | flops 3782040576 | bytes 86758584 | solution.py:393
  433.5 83.2 %conditional.11 = (bf16[256,1024]{1,0:T(8,128)(2,1)S(1)}, bf16[256,2816]{1,0:T(8,128)(2,1)S(1)}) conditional(s32[]{:T(128)} %clamp.31, (bf16[2,256,1024]{2,1,0:T(8,128)(2,1)S(1)}, s32[]{:T(128)}, s32[2,256]{1,0:T(2,128)S(1)}, f32[4,1024]{1,0:T(4,128)S(1)}, bf16[2,3,1024,1024]{3,2,1,0:T(8,128)(2,1)}, ...), branch_computations={%region_13.20_spmd, %region_20.24_spmd, %region_24.26_spmd, %regio... | conditional | flops 3782040576 | bytes 90952920 | solution.py:393
  602.5 25.7 conditional.15
  647.2 26.5 conditional.16
  676.3 24.2 collective-permute-done.10
  700.5 26.4 conditional.17
  729.6 188.7 %collective-permute-done.12 = bf16[256,1024]{1,0:T(8,128)(2,1)S(1)} collective-permute-done((bf16[256,1024]{1,0:T(8,128)(2,1)}, bf16[256,1024]{1,0:T(8,128)(2,1)S(1)}, u32[]{:S(2)}, u32[]{:S(2)}) %collective-permute-start.12) | collective-permute-done | bytes 524320 | tf_op jit(solution)/shard_map/ppermute | solution.py:22
  918.3 320.8 %conditional.18 = (bf16[256,1024]{1,0:T(8,128)(2,1)}, bf16[256,2816]{1,0:T(8,128)(2,1)}, bf16[256,1024]{1,0:T(8,128)(2,1)S(1)}, bf16[640,1024]{1,0:T(8,128)(2,1)}, f32[1024,5634]{1,0:T(8,128)}) conditional(s32[]{:T(128)} %clamp.38, (bf16[2,256,1024]{2,1,0:T(8,128)(2,1)}, s32[]{:T(128)}, f32[4,1024]{1,0:T(4,128)S(1)}, ...), branch_computations={%region_154.168_spmd, %region_168.175_spmd, %region_175.179_spmd, ... | conditional | flops 10853389312 | bytes 450503808 | solution.py:501
  1145.3 51.4 %concatenate.116 = f32[1024,5634]{0,1:T(8,128)} concatenate(f32[1024,5632]{0,1:T(8,128)} %select_maximum_fusion.24, f32[1024,1]{0,1:T(1,128)S(1)} %bitcast.2160, f32[1024,1]{0,1:T(1,128)S(1)} %bitcast.2169), dimensions={1} | concatenate | bytes 46153728 | tf_op jit(solution)/shard_map/cond/branch_0_fun/concatenate | solution.py:345
  1253.1 322.8 %conditional.19 = (bf16[256,1024]{1,0:T(8,128)(2,1)S(1)}, bf16[640,1024]{1,0:T(8,128)(2,1)}, f32[1024,5634]{1,0:T(8,128)}) conditional(s32[]{:T(128)} %clamp.39, (bf16[2,256,1024]{2,1,0:T(8,128)(2,1)}, s32[]{:T(128)}, f32[4,1024]{1,0:T(4,128)S(1)}, s32[2,256]{1,0:T(2,128)S(1)}, bf16[2,3,1024,1024]{3,2,1,0:T(8,128)(2,1)}, ...), branch_computations={%region_181.195_spmd, %region_195.201_spmd, %region_201.204_spmd, ... | conditional | flops 10853389312 | bytes 444343360 | solution.py:501
  1481.7 51.4 %concatenate.121 = f32[1024,5634]{0,1:T(8,128)} concatenate(f32[1024,5632]{0,1:T(8,128)} %select_maximum_fusion.27, f32[1024,1]{0,1:T(1,128)S(1)} %bitcast.2161, f32[1024,1]{0,1:T(1,128)S(1)} %bitcast.2170), dimensions={1} | concatenate | bytes 46153728 | tf_op jit(solution)/shard_map/cond/branch_0_fun/concatenate | solution.py:345
  1533.1 23.8 copy.685
  1575.9 53.0 %broadcast_select_fusion = (f32[1024,5634]{1,0:T(8,128)}, f32[1024,5634]{1,0:T(8,128)}) fusion(pred[]{:T(512)S(6)} %eq.11, f32[1024,5634]{1,0:T(8,128)} %get-tuple-element.1592, f32[1024,5634]{1,0:T(8,128)} %get-tuple-element.1591, f32[1024,5634]{1,0:T(8,128)} %get-tuple-element.1590, f32[1024,5634]{1,0:T(8,128)} %get-tuple-element.1588, ...), kind=kLoop, calls=%fused_computation.1801 | loop fusion | flops 28846080 | bytes 161538048 | tf_op jit(solution)/shard_map/jit(_where)/select_n | solution.py:534
  1754.8 35.8 %reduce-scatter.25.cloned.1.call-done = f32[32,4]{1,0:T(8,128)} async-done(((f32[1024,4]{1,0:T(8,128)}), f32[32,4]{1,0:T(8,128)}) %reduce-scatter.25.cloned.1.call-update) | async-done | bytes 528
  1814.6 28.0 %reduce-scatter.13.cloned.1.call-done = bf16[2,64,1024]{2,1,0:T(8,128)(2,1)} async-done(((bf16[2,256,1024]{2,1,0:T(8,128)(2,1)}), bf16[2,64,1024]{2,1,0:T(8,128)(2,1)}) %reduce-scatter.13.cloned.1.call-update) | async-done | bytes 262160 | tf_op jit(solution)/shard_map/reduce_scatter | solution.py:521
  1842.6 38.0 %reduce-scatter.15.cloned.1.call-done = bf16[2,160,1024]{2,1,0:T(8,128)(2,1)} async-done(((bf16[2,640,1024]{2,1,0:T(8,128)(2,1)}), bf16[2,160,1024]{2,1,0:T(8,128)(2,1)}) %reduce-scatter.15.cloned.1.call-update) | async-done | bytes 655376 | tf_op jit(solution)/shard_map/reduce_scatter | solution.py:527
  1880.6 151.8 %reduce-scatter.19.cloned.1.call-done = f32[2,32,1024]{2,1,0:T(8,128)} async-done(((f32[2,1024,1024]{2,1,0:T(8,128)}), f32[2,32,1024]{2,1,0:T(8,128)}) %reduce-scatter.19.cloned.1.call-update) | async-done | bytes 262160 | tf_op jit(solution)/shard_map/reduce_scatter | solution.py:562
  2032.4 153.5 %reduce-scatter.23.cloned.1.call-done = f32[88,1024]{1,0:T(8,128)} async-done(((f32[2816,1024]{1,0:T(8,128)}), f32[88,1024]{1,0:T(8,128)}) %reduce-scatter.23.cloned.1.call-update) | async-done | bytes 360464 | tf_op jit(solution)/shard_map/reduce_scatter | solution.py:584
  2185.9 250.5 %reduce-scatter.17.cloned.1.call-done = f32[2,3,32,1024]{3,2,1,0:T(8,128)} async-done(((f32[2,3,1024,1024]{3,2,1,0:T(8,128)}), f32[2,3,32,1024]{3,2,1,0:T(8,128)}) %reduce-scatter.17.cloned.1.call-update) | async-done | bytes 786448 | tf_op jit(solution)/shard_map/reduce_scatter | solution.py:539
  2436.4 249.7 %reduce-scatter.21.cloned.1.call-done = f32[2,32,2816]{2,1,0:T(8,128)} async-done(((f32[2,1024,2816]{2,1,0:T(8,128)}), f32[2,32,2816]{2,1,0:T(8,128)}) %reduce-scatter.21.cloned.1.call-update) | async-done | bytes 720912 | tf_op jit(solution)/shard_map/reduce_scatter | solution.py:573
  (503 shorter events, 966.3 us)
Async XLA Ops:
  7.2 98.0 %all-gather.9.cloned.1.call-start = ((), (), s32[]{:S(2)}) async-start(), calls=%async_computation.10 | async-start | bytes 11894784 | tf_op jit(solution)/shard_map/all_gather | solution.py:329
  7.9 160.6 %all-gather.7.cloned.1.call-start = ((), (), s32[]{:S(2)}) async-start(), calls=%async_computation.9 | async-start | bytes 4325376 | tf_op jit(solution)/shard_map/all_gather | solution.py:328
  8.6 257.1 %all-gather.5.cloned.1.call-start = ((), (), s32[]{:S(2)}) async-start(), calls=%async_computation.8 | async-start | bytes 12976128 | tf_op jit(solution)/shard_map/all_gather | solution.py:327
  9.4 324.8 %all-gather.11.cloned.1.call-start = ((), (), s32[]{:S(2)}) async-start(), calls=%async_computation.11 | async-start | bytes 5947392 | tf_op jit(solution)/shard_map/all_gather | solution.py:330
  10.0 1780.7 %reduce-scatter.25.cloned.1.call-start = ((), (), s32[]{:S(2)}) async-start(), calls=%async_computation.19 | async-start | bytes 540672
  422.3 11.0 collective-permute-start.1
  534.9 20.3 collective-permute-start.4
  568.0 30.9 %collective-permute-start.6 = (bf16[256,1024]{1,0:T(8,128)(2,1)}, bf16[256,1024]{1,0:T(8,128)(2,1)S(1)}, u32[]{:S(2)}, u32[]{:S(2)}) collective-permute-start(bf16[256,1024]{1,0:T(8,128)(2,1)} %get-tuple-element.1468), channel_id=1, source_target_pairs={{0,1},{1,2},{2,3},{4,5},{5,6},{6,7},{8,9},{9,10},{10,11},{12,13},{... | collective-permute-start | bytes 1572872 | tf_op jit(solution)/shard_map/ppermute | solution.py:22
  582.6 17.9 collective-permute-start.7
  628.3 18.9 collective-permute-start.9
  629.6 17.6 collective-permute-start.8
  673.7 26.8 collective-permute-start.11
  675.0 25.5 collective-permute-start.10
  726.9 191.4 %collective-permute-start.13 = (bf16[256,2816]{1,0:T(8,128)(2,1)}, bf16[256,2816]{1,0:T(8,128)(2,1)S(1)}, u32[]{:S(2)}, u32[]{:S(2)}) collective-permute-start(bf16[256,2816]{1,0:T(8,128)(2,1)} %get-tuple-element.1478), channel_id=1, source_target_pairs={{1,0},{2,1},{3,2},{5,4},{6,5},{7,6},{9,8},{10,9},{11,10},{13,12},{... | collective-permute-start | bytes 4325384 | tf_op jit(solution)/shard_map/ppermute | solution.py:22
  728.2 190.1 %collective-permute-start.12 = (bf16[256,1024]{1,0:T(8,128)(2,1)}, bf16[256,1024]{1,0:T(8,128)(2,1)S(1)}, u32[]{:S(2)}, u32[]{:S(2)}) collective-permute-start(bf16[256,1024]{1,0:T(8,128)(2,1)} %get-tuple-element.1477), channel_id=1, source_target_pairs={{1,0},{2,1},{3,2},{5,4},{6,5},{7,6},{9,8},{10,9},{11,10},{13,12},{... | collective-permute-start | bytes 1572872 | tf_op jit(solution)/shard_map/ppermute | solution.py:22
  1239.2 13.1 collective-permute-start.15
  1241.2 11.1 collective-permute-start.14
  1657.9 156.7 %reduce-scatter.11.cloned.1.call-start = ((), (), s32[]{:S(2)}) async-start(), calls=%async_computation.12 | async-start | bytes 1310720 | tf_op jit(solution)/shard_map/reduce_scatter | solution.py:515
  1659.2 183.4 %reduce-scatter.13.cloned.1.call-start = ((), (), s32[]{:S(2)}) async-start(), calls=%async_computation.13 | async-start | bytes 1310720 | tf_op jit(solution)/shard_map/reduce_scatter | solution.py:521
  1662.2 218.4 %reduce-scatter.15.cloned.1.call-start = ((), (), s32[]{:S(2)}) async-start(), calls=%async_computation.14 | async-start | bytes 3276800 | tf_op jit(solution)/shard_map/reduce_scatter | solution.py:527
  1670.0 362.4 %reduce-scatter.19.cloned.1.call-start = ((), (), s32[]{:S(2)}) async-start(), calls=%async_computation.16 | async-start | bytes 8650752 | tf_op jit(solution)/shard_map/reduce_scatter | solution.py:562
  1696.3 489.6 %reduce-scatter.23.cloned.1.call-start = ((), (), s32[]{:S(2)}) async-start(), calls=%async_computation.18 | async-start | bytes 11894784 | tf_op jit(solution)/shard_map/reduce_scatter | solution.py:584
  1719.2 717.2 %reduce-scatter.17.cloned.1.call-start = ((), (), s32[]{:S(2)}) async-start(), calls=%async_computation.15 | async-start | bytes 25952256 | tf_op jit(solution)/shard_map/reduce_scatter | solution.py:539
  1738.1 948.0 %reduce-scatter.21.cloned.1.call-start = ((), (), s32[]{:S(2)}) async-start(), calls=%async_computation.17 | async-start | bytes 23789568 | tf_op jit(solution)/shard_map/reduce_scatter | solution.py:573
  (94 other events, 797.4 us)
Sparse Core Ops, SparseCore 0:
  11.0 94.0 all-gather.8
  108.1 60.3 all-gather.6
  171.4 94.2 all-gather.4
  268.5 65.5 all-gather.10
  1658.0 132.5 reduce-scatter.24
  1793.7 20.7 reduce-scatter.10
  1817.7 24.8 reduce-scatter.12
  1845.9 34.6 reduce-scatter.14
  1883.4 148.9 reduce-scatter.18
  2035.1 150.6 reduce-scatter.22
  2192.9 243.4 reduce-scatter.16
  2439.2 246.8 reduce-scatter.20
where the time goes:
time: 2710 us; the launch traced here: 2690 us
  waiting for transfers between devices  1490 us (55%)
  local copies, waits for them, and re-layouts  552 us (20%)
  other arithmetic  370 us (14%)
  loops' own time  113 us (4%)
  matrix products  97.2 us (4%)
  starting transfers between devices  59 us (2%)
    reduce_scatter x1, waiting for transfers between devices, local(): lax.psum_scatter(jnp.stack([jnp.stack([columns_of(cross_part, 0, feature)...  251 us
    reduce_scatter x1, waiting for transfers between devices, local(): lax.psum_scatter(jnp.stack([columns_of(gate_part, 0, hidden_width), colum...  250 us
    ppermute x16, waiting for transfers between devices, shifted(): return lax.ppermute(block, axis, route)  229 us
    reduce_scatter x1, waiting for transfers between devices, local(): lax.psum_scatter(columns_of(masked[3], 0, hidden_width).reshape(-1, featu...  153 us
    reduce_scatter x1, waiting for transfers between devices, local(): lax.psum_scatter(jnp.stack([columns_of(cross_part, 3 * feature, feature),...  152 us
    concatenate x2, local copies, waits for them, and re-layouts, pack_grads(): jnp.concatenate([main, gain_first[:, None], gain_second[:, None]], axis=1)  103 us
    all_gather x1, waiting for transfers between devices, local(): lax.all_gather(attn_weights, ('dp', 'pipe'), axis=2, tiled=True)  97.3 us
    all_gather x1, waiting for transfers between devices, local(): lax.all_gather(gate_up, ('dp', 'pipe'), axis=1, tiled=True)  95.1 us
  transfers between devices with their start and end apart: 28, of which 15 were waited for; matrix products, arithmetic and copies ran while one was open for 4% of the time, Pallas kernels for 0%

commit v1 on v0

v1 whole, which is shorter than its diff:
```python
import jax
import jax.numpy as jnp
from jax import lax
from jax.sharding import PartitionSpec as P

HEADS = 16
HEAD_DIM = 64
EPSILON = 1e-06
NEGATIVE = -1e30
SCALE = HEAD_DIM ** (-0.5)
BF = jnp.bfloat16
F32 = jnp.float32


def dot(left, right, contract):
    return lax.dot_general(left, right, (contract, ((), ())), preferred_element_type=F32)


def product(left, right):
    return dot(left, right, ((1,), (0,)))


def product_left(left, right):
    return dot(left, right, ((0,), (0,)))


def product_right(left, right):
    return dot(left, right, ((1,), (1,)))


def norm_rows(values, gain):
    factor = lax.rsqrt(jnp.mean(values * values, axis=-1, keepdims=True) + EPSILON)
    return (values * factor * gain).astype(BF), factor


def norm_back(values, factor, gain, gradient):
    weighted = gradient * gain
    grad_gain = jnp.sum(gradient * values * factor, axis=0)
    grad_values = factor * weighted - values * factor**3 * jnp.mean(weighted * values, axis=-1, keepdims=True)
    return grad_values, grad_gain


def heads_of(values):
    return values.reshape(values.shape[0], HEADS, HEAD_DIM).transpose(1, 0, 2)


def rows_of(values):
    return values.transpose(1, 0, 2).reshape(values.shape[1], -1).astype(BF)


def batched(left, right, left_dim, right_dim):
    return lax.dot_general(left, right, (((left_dim,), (right_dim,)), ((0,), (0,))), preferred_element_type=F32)


def attend(queries, keys, values, allowed):
    scores = batched(queries, keys, 2, 2) * SCALE
    weights = jax.nn.softmax(jnp.where(allowed[None], scores, NEGATIVE), axis=-1)
    low = weights.astype(BF)
    return weights, low, rows_of(batched(low, values, 2, 1))


def attend_back(queries, keys, values, weights, low, grad_mixed):
    grad_weights = batched(grad_mixed, values, 2, 2)
    grad_scores = weights * (grad_weights - jnp.sum(weights * grad_weights, axis=-1, keepdims=True))
    grad_scores = grad_scores.astype(BF)
    return (
        rows_of(batched(grad_scores, keys, 2, 1) * SCALE),
        rows_of(batched(grad_scores, queries, 1, 1) * SCALE),
        rows_of(batched(low, grad_mixed, 1, 1)),
    )


def local(patch_states, byte_states, cotangent, patch_lengths, row_lengths, attn_weights, out_weights, gate_up, down_weight, gains):
    everyone = ("dp", "pipe")
    micro = patch_states.shape[0]
    stages = lax.axis_size("pipe")
    share = stages // micro
    place = lax.axis_index("pipe")
    row, part = place // share, place % share
    attn = lax.all_gather(attn_weights, everyone, axis=2, tiled=True)
    outw = lax.all_gather(out_weights, everyone, axis=1, tiled=True)
    gate_stack = lax.all_gather(gate_up, everyone, axis=1, tiled=True)
    down = lax.all_gather(down_weight, everyone, axis=0, tiled=True)

    def mine(source):
        return lax.dynamic_index_in_dim(source, row, 0, keepdims=False)

    def half(values):
        count = values.shape[0] // share
        return lax.dynamic_slice_in_dim(values, part * count, count, 0)

    def weight_grad(left, right):
        return product_left(half(left), half(right)).astype(BF)

    patch = mine(patch_states).astype(F32)
    byte = mine(byte_states).astype(F32)
    cot = mine(cotangent)
    sizes = mine(patch_lengths)
    length = mine(row_lengths)
    patches, bytes_ = patch.shape[0], byte.shape[0]

    nq, fq = norm_rows(patch, gains[0])
    nb, fb = norm_rows(byte, gains[1])
    qc = heads_of(product(nq, attn[0, 0]).astype(BF))
    kc = heads_of(product(nb, attn[0, 1]).astype(BF))
    vc = heads_of(product(nb, attn[0, 2]).astype(BF))
    ends = jnp.cumsum(sizes)[:, None]
    position = jnp.arange(bytes_, dtype=jnp.int32)[None, :]
    window = (position >= ends - sizes[:, None]) & (position < ends)
    pc32, pc, oc = attend(qc, kc, vc, window)
    x1 = (patch + product(oc, outw[0])).astype(BF)
    x1f = x1.astype(F32)
    n1, f1 = norm_rows(x1f, gains[2])
    q = heads_of(product(n1, attn[1, 0]).astype(BF))
    k = heads_of(product(n1, attn[1, 1]).astype(BF))
    v = heads_of(product(n1, attn[1, 2]).astype(BF))
    slot = jnp.arange(patches, dtype=jnp.int32)
    allowed = (slot[None, :] <= slot[:, None]) & (slot[None, :] < length)
    a32, a, o = attend(q, k, v, allowed)
    x2 = (x1f + product(o, outw[1])).astype(BF)
    x2f = x2.astype(F32)
    n2, f2 = norm_rows(x2f, gains[3])
    gate = product(n2, gate_stack[0])
    up = product(n2, gate_stack[1])
    sig = jax.nn.sigmoid(gate)
    hidden = (gate * sig * up).astype(BF)
    result = (x2f + product(hidden, down)).astype(BF)

    grad_down = weight_grad(hidden, cot)
    dh = product_right(cot, down).astype(BF).astype(F32)
    dgate = (dh * up * sig * (1.0 + gate * (1.0 - sig))).astype(BF)
    dup = (dh * gate * sig).astype(BF)
    grad_gate_up = jnp.stack([weight_grad(n2, dgate), weight_grad(n2, dup)])
    dn2 = product_right(dgate, gate_stack[0]) + product_right(dup, gate_stack[1])
    back, gain3 = norm_back(x2f, f2, gains[3], dn2)
    dx2 = (cot.astype(F32) + back).astype(BF)
    do = heads_of(product_right(dx2, outw[1]).astype(BF))
    dq, dk, dv = attend_back(q, k, v, a32, a, do)
    dn1 = product_right(dq, attn[1, 0]) + product_right(dk, attn[1, 1]) + product_right(dv, attn[1, 2])
    back, gain2 = norm_back(x1f, f1, gains[2], dn1)
    dx1 = (dx2.astype(F32) + back).astype(BF)
    doc = heads_of(product_right(dx1, outw[0]).astype(BF))
    dqc, dkc, dvc = attend_back(qc, kc, vc, pc32, pc, doc)
    back, gain0 = norm_back(patch, fq, gains[0], product_right(dqc, attn[0, 0]))
    grad_patch = (dx1.astype(F32) + back).astype(BF)
    back, gain1 = norm_back(byte, fb, gains[1], product_right(dkc, attn[0, 1]) + product_right(dvc, attn[0, 2]))
    grad_byte = back.astype(BF)
    grad_attn = jnp.stack(
        [
            jnp.stack([weight_grad(nq, dqc), weight_grad(nb, dkc), weight_grad(nb, dvc)]),
            jnp.stack([weight_grad(n1, dq), weight_grad(n1, dk), weight_grad(n1, dv)]),
        ]
    )
    grad_out = jnp.stack([weight_grad(oc, dx1), weight_grad(o, dx2)])
    grad_gains = jnp.where(part == 0, jnp.stack([gain0, gain1, gain2, gain3]), 0.0)

    def to_owner(values):
        whole = lax.all_gather(half(values), "pipe", axis=0, tiled=True)
        whole = whole.reshape(micro, -1, values.shape[1])
        count = whole.shape[1] // stages
        return lax.dynamic_slice_in_dim(whole, place * count, count, 1)

    def summed(values, axis):
        return lax.psum_scatter(values, everyone, scatter_dimension=axis, tiled=True).astype(F32)

    return (
        to_owner(result),
        to_owner(grad_patch),
        to_owner(grad_byte),
        summed(grad_attn, 2),
        summed(grad_out, 1),
        summed(grad_gate_up, 1),
        summed(grad_down, 0),
        summed(grad_gains, 1),
    )


def solution(mesh):
    placed = (
        P("dp", None, None),
        P("dp", None, None),
        P("dp", None, None),
        P("dp", None),
        P("dp"),
        P(None, None, ("dp", "pipe"), None),
        P(None, ("dp", "pipe"), None),
        P(None, ("dp", "pipe"), None),
        P(("dp", "pipe"), None),
        P(),
    )
    return jax.shard_map(
        local,
        mesh=mesh,
        in_specs=placed,
        out_specs=(
            P("dp", "pipe", None),
            P("dp", "pipe", None),
            P("dp", "pipe", None),
            P(None, None, ("dp", "pipe"), None),
            P(None, ("dp", "pipe"), None),
            P(None, ("dp", "pipe"), None),
            P(("dp", "pipe"), None),
            P(None, ("dp", "pipe")),
        ),
        check_vma=False,
    )
```

time: 2710 us -> 1210 us (0.45)
  local copies, waits for them, and re-layouts: 552 us -> 26.6 us
  waiting for transfers between devices: 1490 us -> 993 us
  other arithmetic: 370 us -> 40 us
  loops' own time: 113 us -> 0 us
  starting transfers between devices: 59 us -> 1.03 us
  matrix products: 97.2 us -> 130 us
    reduce_scatter x7 -> x4, waiting for transfers between devices: 894 us -> 593 us  [summed(): lax.psum_scatter(values, everyone, scatter_dimension=axis, tiled=True)]
    ppermute x16 -> x0, waiting for transfers between devices: 229 us -> none  [shifted(): return lax.ppermute(block, axis, route)]
    reshape x13 -> x0, local copies, waits for them, and re-layouts: 165 us -> none  [the longest x4 46.9 us: cross_state(): key_rows[byte_index].reshape(row_count, PATCH_MAX, HEADS, HEAD_DIM)]
    another operation x10 -> x0, loops' own time: 113 us -> none  [the longest x5 74.3 us: local(): lax.switch(jnp.where(active, section_id, 4), [backward_cross, backward_gl...]
    concatenate x2 -> x0, local copies, waits for them, and re-layouts: 103 us -> none  [pack_grads(): jnp.concatenate([main, gain_first[:, None], gain_second[:, None]], axis=1)]
    scatter-add x4 -> x0, other arithmetic: 82.9 us -> none  [the longest x2 41.5 us: cross_back(): empty_bytes.at[flat_index].add(grad_key_win.reshape(-1, feature))]
    select_n x9 -> x1, other arithmetic: 79.6 us -> 0.02 us  [local(): jnp.where(part == 0, jnp.stack([gain0, gain1, gain2, gain3]), 0.0)]
    gather x8 -> x0, local copies, waits for them, and re-layouts: 78.1 us -> none  [the longest x4 39.5 us: cross_state(): key_rows[byte_index].reshape(row_count, PATCH_MAX, HEADS, HEAD_DIM)]
  transfers between devices with their start and end apart: 28 -> 12, of which waited for: 15 -> 12; matrix products, arithmetic and copies ran while one was open for 4% -> 10% of each run, Pallas kernels for 0% -> 0%
where the time goes in v1:
time: 1210 us
  waiting for transfers between devices  993 us (82%)
  matrix products  130 us (11%)
  other arithmetic  40 us (3%)
  local copies, waits for them, and re-layouts  26.6 us (2%)
  between operations  15.6 us (1%)
    reduce_scatter x4, waiting for transfers between devices, summed(): lax.psum_scatter(values, everyone, scatter_dimension=axis, tiled=True)  593 us
    dot_general x33, matrix products, dot(): lax.dot_general(left, right, (contract, ((), ())), preferred_element_type...  94.5 us
    all_gather x1, waiting for transfers between devices, local(): attn = lax.all_gather(attn_weights, everyone, axis=2, tiled=True)  91.3 us
    unnamed x13, waiting for transfers between devices  88.3 us
    all_gather x1, waiting for transfers between devices, local(): gate_stack = lax.all_gather(gate_up, everyone, axis=1, tiled=True)  74.5 us
    all_gather x3, waiting for transfers between devices, to_owner(): whole = lax.all_gather(half(values), 'pipe', axis=0, tiled=True)  56.8 us
    all_gather x1, waiting for transfers between devices, local(): down = lax.all_gather(down_weight, everyone, axis=0, tiled=True)  56.7 us
    all_gather x1, waiting for transfers between devices, local(): outw = lax.all_gather(out_weights, everyone, axis=1, tiled=True)  32.5 us
  transfers between devices with their start and end apart: 12, of which 12 were waited for; matrix products, arithmetic and copies ran while one was open for 10% of the time, Pallas kernels for 0%

profile of v1, /device:TPU:0, one launch (start us, length us, event | category | flops | bytes accessed | tf_op | source)
XLA Modules:
  0.0 1206.6 jit_solution(2738987788717410538)
XLA Ops:
  18.1 91.3 %all-gather.8.cloned.1.call-done = bf16[2,3,1024,1024]{3,2,1,0:T(8,128)(2,1)} async-done(((bf16[2,3,32,1024]{3,2,1,0:T(8,128)(2,1)}), bf16[2,3,1024,1024]{3,2,1,0:T(8,128)(2,1)}) %all-gather.8.cloned.1.call-update) | async-done | bytes 12582928 | tf_op jit(solution)/shard_map/all_gather | solution.py:80
  127.3 6.9 fusion.157
  134.2 6.0 fusion.61
  140.2 32.5 %all-gather.10.cloned.1.call-done = bf16[2,1024,1024]{2,1,0:T(8,128)(2,1)} async-done(((bf16[2,32,1024]{2,1,0:T(8,128)(2,1)}), bf16[2,1024,1024]{2,1,0:T(8,128)(2,1)}) %all-gather.10.cloned.1.call-update) | async-done | bytes 4194320 | tf_op jit(solution)/shard_map/all_gather | solution.py:81
  191.2 74.5 %all-gather.12.cloned.1.call-done = bf16[2,1024,2816]{2,1,0:T(8,128)(2,1)} async-done(((bf16[2,32,2816]{2,1,0:T(8,128)(2,1)}), bf16[2,1024,2816]{2,1,0:T(8,128)(2,1)}) %all-gather.12.cloned.1.call-update) | async-done | bytes 11534352 | tf_op jit(solution)/shard_map/all_gather | solution.py:82
  265.7 5.8 fusion.7
  271.5 5.9 fusion.9
  277.4 56.7 %all-gather.14.cloned.1.call-done = bf16[2816,1024]{1,0:T(8,128)(2,1)} async-done(((bf16[88,1024]{1,0:T(8,128)(2,1)}), bf16[2816,1024]{1,0:T(8,128)(2,1)}) %all-gather.14.cloned.1.call-update) | async-done | bytes 5767184 | tf_op jit(solution)/shard_map/all_gather | solution.py:83
  334.2 8.4 multiply_convert_fusion.2
  342.6 5.4 fusion.6
  374.6 5.3 fusion.40
  396.1 5.3 multiply_reduce_fusion.2
  404.6 4.7 fusion.159
  419.8 5.4 convolution_convert_fusion
  434.3 5.4 pad_maximum_fusion
  444.6 5.2 pad_maximum_fusion.1
  449.8 85.6 %reduce-scatter.16.cloned.1.call-done = f32[32,4]{1,0:T(8,128)} async-done(((f32[1024,4]{1,0:T(8,128)}), f32[32,4]{1,0:T(8,128)}) %reduce-scatter.16.cloned.1.call-update) | async-done | bytes 528
  536.8 13.4 %all-gather.18.cloned.1.call-done = bf16[512,1024]{1,0:T(8,128)(2,1)} async-done(((bf16[128,1024]{1,0:T(8,128)(2,1)}), bf16[512,1024]{1,0:T(8,128)(2,1)}) %all-gather.18.cloned.1.call-update) | async-done | bytes 1048592 | tf_op jit(solution)/shard_map/all_gather | solution.py:158
  551.9 17.3 %all-gather.16.cloned.1.call-done = bf16[512,1024]{1,0:T(8,128)(2,1)} async-done(((bf16[128,1024]{1,0:T(8,128)(2,1)}), bf16[512,1024]{1,0:T(8,128)(2,1)}) %all-gather.16.cloned.1.call-update) | async-done | bytes 1048592 | tf_op jit(solution)/shard_map/all_gather | solution.py:158
  570.8 26.1 %all-gather.20.cloned.1.call-done = bf16[1280,1024]{1,0:T(8,128)(2,1)} async-done(((bf16[320,1024]{1,0:T(8,128)(2,1)}), bf16[1280,1024]{1,0:T(8,128)(2,1)}) %all-gather.20.cloned.1.call-update) | async-done | bytes 2621456 | tf_op jit(solution)/shard_map/all_gather | solution.py:158
  598.9 141.7 %reduce-scatter.10.cloned.1.call-done = bf16[2,32,1024]{2,1,0:T(8,128)(2,1)} async-done(((bf16[2,1024,1024]{2,1,0:T(8,128)(2,1)}), bf16[2,32,1024]{2,1,0:T(8,128)(2,1)}) %reduce-scatter.10.cloned.1.call-update) | async-done | bytes 131088 | tf_op jit(solution)/shard_map/reduce_scatter | solution.py:164
  742.2 140.3 %reduce-scatter.14.cloned.1.call-done = bf16[88,1024]{1,0:T(8,128)(2,1)} async-done(((bf16[2816,1024]{1,0:T(8,128)(2,1)}), bf16[88,1024]{1,0:T(8,128)(2,1)}) %reduce-scatter.14.cloned.1.call-update) | async-done | bytes 180240 | tf_op jit(solution)/shard_map/reduce_scatter | solution.py:164
  884.2 156.9 %reduce-scatter.8.cloned.1.call-done = bf16[2,3,32,1024]{3,2,1,0:T(8,128)(2,1)} async-done(((bf16[2,3,1024,1024]{3,2,1,0:T(8,128)(2,1)}), bf16[2,3,32,1024]{3,2,1,0:T(8,128)(2,1)}) %reduce-scatter.8.cloned.1.call-update) | async-done | bytes 393232 | tf_op jit(solution)/shard_map/reduce_scatter | solution.py:164
  1043.1 154.3 %reduce-scatter.12.cloned.1.call-done = bf16[2,32,2816]{2,1,0:T(8,128)(2,1)} async-done(((bf16[2,1024,2816]{2,1,0:T(8,128)(2,1)}), bf16[2,32,2816]{2,1,0:T(8,128)(2,1)}) %reduce-scatter.12.cloned.1.call-update) | async-done | bytes 360464 | tf_op jit(solution)/shard_map/reduce_scatter | solution.py:164
  (221 shorter events, 130.5 us)
Async XLA Ops:
  7.2 102.3 %copy-start.7 = (bf16[2,640,1024]{2,1,0:T(8,128)(2,1)S(1)}, bf16[2,640,1024]{2,1,0:T(8,128)(2,1)}, u32[]{:S(2)}) copy-start(bf16[2,640,1024]{2,1,0:T(8,128)(2,1)} %param.11) | copy-start | bytes 7864324
  7.2 10.6 copy-start.38
  7.2 102.3 %all-gather.8.cloned.1.call-start = ((), (), s32[]{:S(2)}) async-start(), calls=%async_computation.5 | async-start | bytes 12976128 | tf_op jit(solution)/shard_map/all_gather | solution.py:80
  7.9 164.8 %all-gather.10.cloned.1.call-start = ((), (), s32[]{:S(2)}) async-start(), calls=%async_computation.6 | async-start | bytes 4325376 | tf_op jit(solution)/shard_map/all_gather | solution.py:81
  8.7 257.0 %all-gather.12.cloned.1.call-start = ((), (), s32[]{:S(2)}) async-start(), calls=%async_computation.7 | async-start | bytes 11894784 | tf_op jit(solution)/shard_map/all_gather | solution.py:82
  9.4 324.7 %all-gather.14.cloned.1.call-start = ((), (), s32[]{:S(2)}) async-start(), calls=%async_computation.8 | async-start | bytes 5947392 | tf_op jit(solution)/shard_map/all_gather | solution.py:83
  10.0 525.4 %reduce-scatter.16.cloned.1.call-start = ((), (), s32[]{:S(2)}) async-start(), calls=%async_computation.16 | async-start | bytes 540672
  127.2 7.0 copy-start.17
  140.2 35.1 %copy-start.31 = (bf16[16,256,64]{1,2,0:T(8,128)(2,1)}, bf16[16,256,64]{1,2,0:T(8,128)(2,1)S(1)}, u32[]{:S(2)}) copy-start(bf16[16,256,64]{1,2,0:T(8,128)(2,1)S(1)} %fusion.61) | copy-start | bytes 1572868
  191.2 80.3 %copy-start.9 = (bf16[256,1024]{1,0:T(8,128)(2,1)}, bf16[256,1024]{1,0:T(8,128)(2,1)S(1)}, u32[]{:S(2)}) copy-start(bf16[256,1024]{1,0:T(8,128)(2,1)S(1)} %fusion.68) | copy-start | bytes 1572868
  353.1 15.6 %copy-start.5 = (bf16[256,1024]{1,0:T(8,128)(2,1)}, bf16[256,1024]{1,0:T(8,128)(2,1)S(1)}, u32[]{:S(2)}) copy-start(bf16[256,1024]{1,0:T(8,128)(2,1)S(1)} %fusion.72) | copy-start | bytes 1572868
  369.8 10.1 slice-start
  374.6 6.6 slice-start.2
  374.6 6.9 copy-start.18
  374.6 7.0 copy-start.26
  381.6 14.4 %copy-start.42 = (bf16[16,640,64]{1,2,0:T(8,128)(2,1)}, bf16[16,640,64]{1,2,0:T(8,128)(2,1)S(1)}, u32[]{:S(2)}) copy-start(bf16[16,640,64]{1,2,0:T(8,128)(2,1)S(1)} %fusion.40) | copy-start | bytes 3932164
  402.4 147.8 %all-gather.18.cloned.1.call-start = ((), (), s32[]{:S(2)}) async-start(), calls=%async_computation.10 | async-start | bytes 1310720 | tf_op jit(solution)/shard_map/all_gather | solution.py:158
  404.5 164.7 %all-gather.16.cloned.1.call-start = ((), (), s32[]{:S(2)}) async-start(), calls=%async_computation.9 | async-start | bytes 1310720 | tf_op jit(solution)/shard_map/all_gather | solution.py:158
  410.2 186.8 %all-gather.20.cloned.1.call-start = ((), (), s32[]{:S(2)}) async-start(), calls=%async_computation.11 | async-start | bytes 3276800 | tf_op jit(solution)/shard_map/all_gather | solution.py:158
  414.6 326.0 %reduce-scatter.10.cloned.1.call-start = ((), (), s32[]{:S(2)}) async-start(), calls=%async_computation.13 | async-start | bytes 4325376 | tf_op jit(solution)/shard_map/reduce_scatter | solution.py:164
  419.5 463.0 %reduce-scatter.14.cloned.1.call-start = ((), (), s32[]{:S(2)}) async-start(), calls=%async_computation.15 | async-start | bytes 5947392 | tf_op jit(solution)/shard_map/reduce_scatter | solution.py:164
  425.3 615.8 %reduce-scatter.8.cloned.1.call-start = ((), (), s32[]{:S(2)}) async-start(), calls=%async_computation.12 | async-start | bytes 12976128 | tf_op jit(solution)/shard_map/reduce_scatter | solution.py:164
  439.7 757.6 %reduce-scatter.12.cloned.1.call-start = ((), (), s32[]{:S(2)}) async-start(), calls=%async_computation.14 | async-start | bytes 11894784 | tf_op jit(solution)/shard_map/reduce_scatter | solution.py:164
  550.2 649.0 %copy-start.1 = (s32[2,256]{1,0:T(2,128)S(1)}, s32[2,256]{1,0:T(2,128)}, u32[]{:S(2)}) copy-start(s32[2,256]{1,0:T(2,128)} %param.13) | copy-start | bytes 6148
  (38 other events, 114.2 us)
Sparse Core Ops, SparseCore 0:
  11.0 98.4 all-gather.7
  112.4 60.2 all-gather.9
  175.8 89.8 all-gather.11
  268.4 65.6 all-gather.13
  402.6 132.8 reduce-scatter.15
  537.5 12.6 all-gather.17
  552.4 16.7 all-gather.15
  571.4 25.5 all-gather.19
  599.4 141.2 reduce-scatter.9
  742.8 139.6 reduce-scatter.13
  889.6 151.4 reduce-scatter.7
  1043.3 154.0 reduce-scatter.11

commit v2 on v1

--- a/solution.py
+++ b/solution.py
@@ -1,6 +1,11 @@
+import functools
+from types import SimpleNamespace
+
 import jax
 import jax.numpy as jnp
 from jax import lax
+from jax.experimental import pallas as pl
+from jax.experimental.pallas import tpu as pltpu
 from jax.sharding import PartitionSpec as P
 
 HEADS = 16
@@ -10,6 +15,7 @@
 SCALE = HEAD_DIM ** (-0.5)
 BF = jnp.bfloat16
 F32 = jnp.float32
+MESH = pl.DeviceIdType.MESH
 
 
 def dot(left, right, contract):
@@ -70,7 +76,7 @@
     )
 
 
-def local(patch_states, byte_states, cotangent, patch_lengths, row_lengths, attn_weights, out_weights, gate_up, down_weight, gains):
+def gathered_step(patch_states, byte_states, cotangent, patch_lengths, row_lengths, attn_weights, out_weights, gate_up, down_weight, gains):
     everyone = ("dp", "pipe")
     micro = patch_states.shape[0]
     stages = lax.axis_size("pipe")
@@ -175,6 +181,910 @@
     )
 
 
+LINE = 4
+SIDE = 2
+RANKS = 4
+GROUPS = LINE * SIDE
+ROWS_HERE = 2
+PATCHES = 256
+BYTES = 640
+WIDTH = 1024
+MINE = WIDTH // RANKS
+HEADS_MINE = MINE // HEAD_DIM
+TOKENS = PATCHES // RANKS
+TOKENS_B = BYTES // RANKS
+SHARD = WIDTH // (GROUPS * RANKS)
+SEG = SHARD * RANKS
+UNITS = 88
+PADDED = 96
+HIDDEN = GROUPS * PADDED
+NSEM = 512
+BIG = (("attn0", 0), ("attn1", 1))
+
+
+def scratch_plan():
+    b = lambda *shape: pltpu.VMEM(shape, BF)
+    f = lambda *shape: pltpu.VMEM(shape, F32)
+    plan = dict(
+        sem=pltpu.SemaphoreType.DMA((NSEM,)),
+        wa=b(6, WIDTH, MINE),
+        won=b(2, LINE, SIDE, SHARD, WIDTH),
+        woh=b(2, 2, 2, HEAD_DIM, WIDTH),
+        wg=b(WIDTH, 2 * HIDDEN),
+        wd=b(HIDDEN, WIDTH),
+        da=b(6, WIDTH, MINE),
+        don=b(2, GROUPS, SHARD, WIDTH),
+        dg=b(WIDTH, 2 * HIDDEN),
+        dd=b(HIDDEN, WIDTH),
+        xa=b(6, LINE, SEG, MINE),
+        xo=b(2, LINE, SHARD, WIDTH),
+        xg=b(LINE, SEG, 2 * HIDDEN),
+        xd=b(LINE, PADDED, WIDTH),
+        za=b(6, LINE + 1, SEG, MINE),
+        zo=b(2, LINE + 1, SHARD, WIDTH),
+        zg=b(LINE + 1, SEG, 2 * HIDDEN),
+        zd=b(LINE + 1, PADDED, WIDTH),
+        nq=b(ROWS_HERE, PATCHES, WIDTH),
+        nb=b(ROWS_HERE, BYTES, WIDTH),
+        qc=b(ROWS_HERE, PATCHES, MINE),
+        kc=b(ROWS_HERE, BYTES, MINE),
+        vc=b(ROWS_HERE, BYTES, MINE),
+        oc=b(ROWS_HERE, PATCHES, MINE),
+        x1=b(8, TOKENS, WIDTH),
+        n1=b(ROWS_HERE, PATCHES, WIDTH),
+        qkv=b(3, ROWS_HERE, PATCHES, MINE),
+        o=b(ROWS_HERE, PATCHES, MINE),
+        x2=b(8, TOKENS, WIDTH),
+        n2=b(ROWS_HERE, PATCHES, WIDTH),
+        fac=b(ROWS_HERE, PATCHES, 2 * HIDDEN),
+        hid=b(ROWS_HERE, PATCHES, HIDDEN),
+        dx2=b(8, TOKENS, WIDTH),
+        dx1=b(8, TOKENS, WIDTH),
+        dmix=b(ROWS_HERE, PATCHES, MINE),
+        dqkv=b(3, ROWS_HERE, PATCHES, MINE),
+        dqc=b(ROWS_HERE, PATCHES, MINE),
+        dkc=b(ROWS_HERE, BYTES, MINE),
+        dvc=b(ROWS_HERE, BYTES, MINE),
+        p=b(8, TOKENS, WIDTH),
+        r1=b(ROWS_HERE, 2, TOKENS, WIDTH),
+        q2=b(ROWS_HERE, TOKENS, WIDTH),
+        r2=b(ROWS_HERE, TOKENS, WIDTH),
+        bp=b(8, TOKENS_B, WIDTH),
+        br1=b(ROWS_HERE, 2, TOKENS_B, WIDTH),
+        bq2=b(ROWS_HERE, TOKENS_B, WIDTH),
+        br2=b(ROWS_HERE, TOKENS_B, WIDTH),
+        bown=b(ROWS_HERE, TOKENS_B, WIDTH),
+        gn=f(8, WIDTH),
+        gs=f(5, 8, WIDTH),
+        gr=f(5, 8, WIDTH),
+    )
+    return plan
+
+
+INS = ("patch", "byte", "cot", "lens", "gains", "wa_in", "wg_in", "wo_in", "wd_in")
+OUTS = ("out", "gpatch", "gbyte", "g_attn", "g_out", "g_gate", "g_down", "g_gain")
+
+
+def step_kernel(names, *refs):
+    m = SimpleNamespace(**dict(zip(INS + OUTS + tuple(names), refs)))
+    dp, pipe = lax.axis_index("dp"), lax.axis_index("pipe")
+    z, x, y, c = dp // SIDE, dp % SIDE, pipe // 2, pipe % 2
+    at = lambda z, x, y, c: (z * SIDE + x, y * 2 + c)
+    sibling, across, aside = at(z, x, y, 1 - c), at(z, x, 1 - y, c), at(z, 1 - x, y, c)
+    right, left = at((z + 1) % LINE, x, y, c), at((z + LINE - 1) % LINE, x, y, c)
+    corner, mirror, pair = at(z, x, 1 - y, 1 - c), at(LINE - 1 - z, x, y, c), at(z + 1 - 2 * (z % 2), x, y, c)
+    counter = [0]
+
+    def take(count=1):
+        first = counter[0]
+        counter[0] += count
+        assert counter[0] <= NSEM
+        return first
+
+    unfinished = []
+
+    def remote(src, dst, device, send=None, recv=None):
+        send = take() if send is None else send
+        recv = take() if recv is None else recv
+        return pltpu.make_async_remote_copy(
+            src_ref=src, dst_ref=dst, send_sem=m.sem.at[send], recv_sem=m.sem.at[recv], device_id=device, device_id_type=MESH
+        )
+
+    def begin(copy):
+        copy.start()
+        unfinished.append(copy.wait_send)
+        return copy
+
+    def near(src, dst):
+        copy = pltpu.make_async_copy(src, dst, m.sem.at[take()])
+        copy.start()
+        return copy
+
+    barrier = pltpu.get_barrier_semaphore()
+    for device in (sibling, across, corner, aside, mirror):
+        pl.semaphore_signal(barrier, inc=1, device_id=device, device_id_type=MESH)
+
+    @pl.when(z < LINE - 1)
+    def _():
+        pl.semaphore_signal(barrier, inc=1, device_id=right, device_id_type=MESH)
+
+    @pl.when(z > 0)
+    def _():
+        pl.semaphore_signal(barrier, inc=1, device_id=left, device_id_type=MESH)
+
+    bytes_in = near(m.byte, m.bp)
+    local_out = near(m.wo_in, m.won.at[:, z, x])
+    local_down = near(m.wd_in, m.wd.at[pl.ds(dp * PADDED, PADDED)])
+    pl.semaphore_wait(barrier, 5 + (z < LINE - 1).astype(jnp.int32) + (z > 0).astype(jnp.int32))
+
+    def attn_part(layer):
+        src = lambda q: m.wa_in.at[q, pl.ds(3 * layer, 3)]
+        dst = m.wa.at[pl.ds(3 * layer, 3), pl.ds(dp * SEG + pipe * SHARD, SHARD)]
+        return src, dst
+
+    def gate_part():
+        return (lambda q: m.wg_in.at[q]), m.wg.at[pl.ds(dp * SEG + pipe * SHARD, SHARD)]
+
+    def spread(part):
+        src, dst = part
+        copies = [near(src(pipe), dst)]
+        for device in (across, corner, sibling):
+            copies.append(begin(remote(src(device[1]), dst, device)))
+        return copies
+
+    def arrived(copies):
+        copies[0].wait()
+        for copy in copies[1:]:
+            copy.wait_recv()
+
+    exchange0, exchange1 = spread(attn_part(0)), spread(attn_part(1))
+    exchange2 = spread(gate_part())
+
+    class Gather:
+        def __init__(self, view):
+            self.view = view
+            self.sx, self.rx = take(LINE), take(LINE)
+            self.sr, self.rr = take(LINE), take(LINE)
+            self.sl, self.rl = take(LINE), take(LINE)
+
+        def copy(self, block, device, send, recv):
+            there = self.view(block * SIDE + x)
+            return remote(there, there, device, send + block, recv + block)
+
+        def aside(self, block):
+            return self.copy(block, aside, self.sx, self.rx)
+
+        def right(self, block):
+            return self.copy(block, right, self.sr, self.rr)
+
+        def left(self, block):
+            return self.copy(block, left, self.sl, self.rl)
+
+        def start(self):
+            self.aside(z).start()
+
+            @pl.when(z < LINE - 1)
+            def _():
+                self.right(z).start()
+
+            @pl.when(z > 0)
+            def _():
+                self.left(z).start()
+
+        def hop(self, k):
+            @pl.when(z - k >= 0)
+            def _():
+                self.right(z - k).wait_recv()
+                self.aside(z - k).start()
+
+                @pl.when(z < LINE - 1)
+                def _():
+                    self.right(z - k).start()
+
+            @pl.when(z + k < LINE)
+            def _():
+                self.left(z + k).wait_recv()
+                self.aside(z + k).start()
+
+                @pl.when(z > 0)
+                def _():
+                    self.left(z + k).start()
+
+        def ready(self):
+            for block in range(LINE):
+                self.aside(block).wait_recv()
+
+        def finish(self):
+            for block in range(LINE):
+                self.aside(block).wait_send()
+
+                @pl.when((z < LINE - 1) & (z >= block))
+                def _():
+                    self.right(block).wait_send()
+
+                @pl.when((z > 0) & (z <= block))
+                def _():
+                    self.left(block).wait_send()
+
+    g_out0 = Gather(lambda d: m.won.at[0, d // SIDE, d % SIDE])
+    g_out1 = Gather(lambda d: m.won.at[1, d // SIDE, d % SIDE])
+    g_attn0 = Gather(lambda d: m.wa.at[pl.ds(0, 3), pl.ds(d * SEG, SEG)])
+    g_attn1 = Gather(lambda d: m.wa.at[pl.ds(3, 3), pl.ds(d * SEG, SEG)])
+    g_gate = Gather(lambda d: m.wg.at[pl.ds(d * SEG, SEG)])
+    g_down = Gather(lambda d: m.wd.at[pl.ds(d * PADDED, PADDED)])
+
+    def begin_after(copies, gather):
+        arrived(copies)
+        gather.start()
+
+    queue = []
+
+    def pump(count):
+        for _ in range(min(count, len(queue))):
+            queue.pop(0)()
+
+    def swap_out(layer):
+        mine, there = m.won.at[layer, pl.ds(2 * c, 2)], m.woh.at[layer, :, :, pl.ds(c * SHARD, SHARD)]
+        keep = near(mine, there)
+        give = remote(m.won.at[layer, pl.ds(2 * (1 - c), 2)], there, sibling)
+        give.start()
+        return keep, give
+
+    lane = lax.broadcasted_iota(jnp.int32, (1, MINE), 1) // HEAD_DIM
+    head_mask = [(lane == j).astype(F32).astype(BF) for j in range(HEADS_MINE)]
+
+    def gain(index):
+        return m.gains[index : index + 1, :]
+
+    def factor_of(values):
+        return lax.rsqrt(jnp.mean(values * values, axis=-1, keepdims=True) + EPSILON)
+
+    def normed(values, index):
+        values = values.astype(F32)
+        return (values * factor_of(values) * gain(index)).astype(BF)
+
+    def norm_back(values, gradient, index):
+        values = values.astype(F32)
+        factor = factor_of(values)
+        weighted = gradient * gain(index)
+        m.gn[index : index + 1, :] += jnp.sum(gradient * values * factor, axis=0, keepdims=True)
+        return factor * weighted - values * (factor * factor * factor) * jnp.mean(weighted * values, axis=-1, keepdims=True)
+
+    def normed_rows(src, dst, index, r):
+        for part in range(RANKS):
+            for half in range(2):
+                rows = pl.ds(half * (TOKENS // 2), TOKENS // 2)
+                dst[r, pl.ds(part * TOKENS + half * (TOKENS // 2), TOKENS // 2)] = normed(src[4 * r + part, rows], index)
+
+    class Reduce:
+        def __init__(self, p, r1, q2, r2, tokens):
+            self.p, self.r1, self.q2, self.r2, self.tokens = p, r1, q2, r2, tokens
+            self.first, self.second = {}, {}
+
+        def give(self, r):
+            self.first[r] = [
+                remote(self.p.at[4 * r + 2 * side + 1 - c], self.r1.at[r, side], sibling) for side in range(2)
+            ]
+            for copy in self.first[r]:
+                copy.start()
+
+        def cross(self, r):
+            for copy in self.first[r]:
+                copy.wait_recv()
+            other = 4 * r + 2 * (1 - y) + c
+            self.q2[r] = (self.p[other].astype(F32) + self.r1[r, 1 - y].astype(F32)).astype(BF)
+            self.second[r] = remote(self.q2.at[r], self.r2.at[r], across)
+            self.second[r].start()
+
+        def arrive(self, r):
+            self.second[r].wait_recv()
+
+        def free(self):
+            for r in range(ROWS_HERE):
+                for copy in self.first[r]:
+                    copy.wait_send()
+                self.second[r].wait_send()
+
+        def total(self, r, rows):
+            own = 4 * r + pipe
+            return (
+                self.p[own, rows].astype(F32) + self.r1[r, y, rows].astype(F32) + self.r2[r, rows].astype(F32)
+            )
+
+    class Share:
+        def __init__(self, values):
+            self.values, self.copies, self.last = values, {}, {}
+
+        def give(self, r):
+            there = self.values.at[4 * r + pipe]
+            self.copies[r] = [begin(remote(there, there, across)), begin(remote(there, there, sibling))]
+
+        def relay(self, r):
+            self.copies[r][0].wait_recv()
+            there = self.values.at[4 * r + 2 * (1 - y) + c]
+            self.last[r] = begin(remote(there, there, sibling))
+
+        def ready(self, r):
+            self.copies[r][1].wait_recv()
+            self.last[r].wait_recv()
+
+    halves = [pl.ds(h * (TOKENS // 2), TOKENS // 2) for h in range(2)]
+
+    def to_owner(reduce, left_of, right_ref, r, right_transposed=False):
+        for n in range(4):
+            cols = pl.ds(n * 256, 256)
+            reduce.p[4 * r : 4 * r + 4, :, cols] = left_of(r, n).astype(BF).reshape(4, reduce.tokens, 256)
+        reduce.give(r)
+
+    queue_start = [
+        lambda: (local_out.wait(), g_out0.start()),
+        lambda: begin_after(exchange0, g_attn0),
+    ]
+    for step in queue_start:
+        step()
+    m.gn[...] = jnp.zeros_like(m.gn)
+
+    @pl.loop(0, ROWS_HERE * PATCHES // 32)
+    def _(i):
+        rows = pl.ds((i % 8) * 32, 32)
+        m.nq[i // 8, rows] = normed(m.patch[i // 8, rows], 0)
+
+    bytes_in.wait()
+
+    @pl.loop(0, 8)
+    def _(i):
+        for part in range(5):
+            rows = pl.ds(part * 32, 32)
+            m.nb[i // 4, pl.ds((i % 4) * TOKENS_B + part * 32, 32)] = normed(m.bp[i, rows], 1)
+
+    def hops(gather):
+        return [functools.partial(gather.hop, k) for k in (1, 2, 3)]
+
+    h_out0, h_attn0, h_out1, h_attn1, h_gate, h_down = map(hops, (g_out0, g_attn0, g_out1, g_attn1, g_gate, g_down))
+    queue += [h_out0[0], g_out1.start, h_attn0[0], h_out0[1], h_attn0[1], h_out0[2]]
+    queue += [lambda: begin_after(exchange1, g_attn1), h_attn0[2]]
+    pump(8)
+    queue += [h_out1[0], h_attn1[0], h_out1[1], lambda: begin_after(exchange2, g_gate), h_attn1[1], h_out1[2], h_attn1[2]]
+    queue += [lambda: (local_down.wait(), g_down.start()), h_gate[0], h_gate[1], h_gate[2]] + h_down
+    g_out0.ready()
+    swap0 = swap_out(0)
+    g_attn0.ready()
+
+    for r in range(ROWS_HERE):
+        m.qc[r] = product(m.nq[r], m.wa[0]).astype(BF)
+
+    @pl.loop(0, 4)
+    def _(i):
+        rows = pl.ds((i % 2) * (BYTES // 2), BYTES // 2)
+        block = m.nb[i // 2, rows]
+        m.kc[i // 2, rows] = product(block, m.wa[1]).astype(BF)
+        m.vc[i // 2, rows] = product(block, m.wa[2]).astype(BF)
+
+    pump(2)
+
+    def window(r):
+        sizes = m.lens[pl.ds(r, 1), :]
+        i = lax.broadcasted_iota(jnp.int32, (PATCHES, PATCHES), 0)
+        j = lax.broadcasted_iota(jnp.int32, (PATCHES, PATCHES), 1)
+        first = jnp.sum(jnp.where(j < i, sizes, 0.0), axis=1, keepdims=True)
+        last = jnp.sum(jnp.where(j <= i, sizes, 0.0), axis=1, keepdims=True)
+        position = lax.broadcasted_iota(jnp.int32, (PATCHES, BYTES), 1).astype(F32)
+        return (position >= first) & (position < last)
+
+    def causal(r):
+        length = m.lens[pl.ds(ROWS_HERE + r, 1), :]
+        i = lax.broadcasted_iota(jnp.int32, (PATCHES, PATCHES), 0)
+        j = lax.broadcasted_iota(jnp.int32, (PATCHES, PATCHES), 1)
+        return (j <= i) & (j.astype(F32) < length)
+
+    def weights_of(query, keys, allowed):
+        scores = jnp.where(allowed, product_right(query, keys) * SCALE, NEGATIVE)
+        raised = jnp.exp(scores - jnp.max(scores, axis=-1, keepdims=True))
+        return raised / jnp.sum(raised, axis=-1, keepdims=True)
+
+    def attend(r, allowed, queries, keys, values, mixed):
+        total = None
+        for j in range(HEADS_MINE):
+            low = weights_of(queries[r] * head_mask[j], keys[r], allowed).astype(BF)
+            term = product(low, values[r] * head_mask[j])
+            total = term if total is None else total + term
+        mixed[r] = total.astype(BF)
+
+    def attend_back(r, allowed, queries, keys, values, grad, dq, dk, dv):
+        sums = [None, None, None]
+        for j in range(HEADS_MINE):
+            query, mixed = queries[r] * head_mask[j], grad[r] * head_mask[j]
+            weights = weights_of(query, keys[r], allowed)
+            grad_weights = product_right(mixed, values[r])
+            grad_scores = weights * (grad_weights - jnp.sum(weights * grad_weights, axis=-1, keepdims=True))
+            grad_scores = grad_scores.astype(BF)
+            terms = (
+                product(grad_scores, keys[r] * head_mask[j]),
+                product_left(grad_scores, query),
+                product_left(weights.astype(BF), mixed),
+            )
+            sums = [t if s is None else s + t for s, t in zip(sums, terms)]
+        dq[r] = (sums[0] * SCALE).astype(BF)
+        dk[r] = (sums[1] * SCALE).astype(BF)
+        dv[r] = sums[2].astype(BF)
+
+    @pl.loop(0, ROWS_HERE)
+    def _(r):
+        attend(r, window(r), m.qc, m.kc, m.vc, m.oc)
+
+    pump(2)
+    for copy in swap0[:1]:
+        copy.wait()
+    swap0[1].wait_recv()
+
+    def out_rows(layer):
+        return lambda n: m.woh[layer, :, :, :, pl.ds(n * 256, 256)].reshape(MINE, 256)
+
+    def residual(reduce, share, base, result, r):
+        reduce.arrive(r)
+        for rows in halves:
+            result[4 * r + pipe, rows] = (base(r, rows) + reduce.total(r, rows)).astype(BF)
+        share.give(r)
+
+    first_sum, first_share = Reduce(m.p, m.r1, m.q2, m.r2, TOKENS), Share(m.x1)
+    for r in range(ROWS_HERE):
+        to_owner(first_sum, lambda r, n: product(m.oc[r], out_rows(0)(n)), None, r)
+    for r in range(ROWS_HERE):
+        first_sum.cross(r)
+    own_patch = lambda r, rows: m.patch[r, pl.ds(pipe * TOKENS + rows.start, TOKENS // 2)].astype(F32)
+    for r in range(ROWS_HERE):
+        residual(first_sum, first_share, own_patch, m.x1, r)
+    pump(2)
+    for r in range(ROWS_HERE):
+        first_share.relay(r)
+    for r in range(ROWS_HERE):
+        first_share.ready(r)
+        normed_rows(m.x1, m.n1, 2, r)
+
+    pump(2)
+    g_out1.ready()
+    swap1 = swap_out(1)
+    g_attn1.ready()
+    for r in range(ROWS_HERE):
+        for part in range(3):
+            m.qkv[part, r] = product(m.n1[r], m.wa[3 + part]).astype(BF)
+    queries, keys, values = m.qkv.at[0], m.qkv.at[1], m.qkv.at[2]
+
+    @pl.loop(0, ROWS_HERE)
+    def _(r):
+        attend(r, causal(r), queries, keys, values, m.o)
+
+    swap1[0].wait()
+    swap1[1].wait_recv()
+    first_sum.free()
+    second_sum, second_share = Reduce(m.p, m.r1, m.q2, m.r2, TOKENS), Share(m.x2)
+    for r in range(ROWS_HERE):
+        to_owner(second_sum, lambda r, n: product(m.o[r], out_rows(1)(n)), None, r)
+    for r in range(ROWS_HERE):
+        second_sum.cross(r)
+    own_of = lambda values: lambda r, rows: values[4 * r + pipe, rows].astype(F32)
+    for r in range(ROWS_HERE):
+        residual(second_sum, second_share, own_of(m.x1), m.x2, r)
+    pump(1)
+    for r in range(ROWS_HERE):
+        second_share.relay(r)
+    for r in range(ROWS_HERE):
+        second_share.ready(r)
+        normed_rows(m.x2, m.n2, 3, r)
+
+    pump(2)
+    g_gate.ready()
+    tiles = HIDDEN // 256
+    for r in range(ROWS_HERE):
+
+        @pl.loop(0, tiles)
+        def _(n, r=r):
+            first = pl.ds(pl.multiple_of(n * 256, 256), 256)
+            later = pl.ds(pl.multiple_of(HIDDEN + n * 256, 256), 256)
+            gate = product(m.n2[r], m.wg[:, first])
+            up = product(m.n2[r], m.wg[:, later])
+            sig = jax.nn.sigmoid(gate)
+            silu = gate * sig
+            m.hid[r, :, first] = (silu * up).astype(BF)
+            m.fac[r, :, first] = (up * sig * (1.0 + gate * (1.0 - sig))).astype(BF)
+            m.fac[r, :, later] = silu.astype(BF)
+
+    class Scatter:
+        def __init__(self, mine, xbuf, zbuf, rows):
+            self.mine, self.xbuf, self.zbuf, self.rows = mine, xbuf, zbuf, rows
+            self.sx, self.rx = take(LINE), take(LINE)
+            self.sr, self.rr = take(LINE), take(LINE)
+            self.sl, self.rl = take(LINE), take(LINE)
+
+        def aside(self, block):
+            return remote(self.mine(block * SIDE + 1 - x), self.xbuf(block), aside, self.sx + block, self.rx + block)
+
+        def start(self):
+            for block in (3, 0, 2, 1):
+                self.aside(block).start()
+
+        def add(self, into, values):
+            into[...] = (into[...].astype(F32) + values[...].astype(F32)).astype(BF)
+
+        def add_x(self, block):
+            self.aside(block).wait_recv()
+            self.add(self.mine(block * SIDE + x), self.xbuf(block))
+
+        def right(self, block):
+            return remote(self.mine(block * SIDE + x), self.zbuf(block), right, self.sr + block, self.rr + block)
+
+        def left(self, block, slot):
+            return remote(self.mine(block * SIDE + x), self.zbuf(slot), left, self.sl + block, self.rl + block)
+
+        def go_right(self, block):
+            @pl.when((z > 0) & (z <= block))
+            def _():
+                self.right(block).wait_recv()
+                self.add(self.mine(block * SIDE + x), self.zbuf(block))
+
+            @pl.when(z < block)
+            def _():
+                self.right(block).start()
+
+        def go_left(self, block):
+            @pl.when((z < LINE - 1) & (z >= block))
+            def _():
+                slot = jnp.where(z == block, LINE, block)
+                self.left(block, slot).wait_recv()
+                self.add(self.mine(block * SIDE + x), self.zbuf(slot))
+
+            @pl.when(z > block)
+            def _():
+                self.left(block, jnp.where(z - 1 == block, LINE, block)).start()
+
+        def steps(self):
+            take_x = lambda block: functools.partial(self.add_x, block)
+            return [
+                lambda: (self.add_x(3), self.go_right(3)),
+                lambda: (self.add_x(0), self.go_left(0)),
+                lambda: (self.add_x(2), self.go_right(2)),
+                lambda: (self.add_x(1), self.go_left(1)),
+                lambda: (self.go_right(1), self.go_left(2)),
+            ]
+
+        def finish(self):
+            for block in range(LINE):
+                self.aside(block).wait_send()
+
+                @pl.when(z < block)
+                def _():
+                    self.right(block).wait_send()
+
+                @pl.when(z > block)
+                def _():
+                    self.left(block, 0).wait_send()
+
+    s_down = Scatter(lambda d: m.dd.at[pl.ds(d * PADDED, PADDED)], lambda b: m.xd.at[b], lambda b: m.zd.at[b], PADDED)
+
+    @pl.loop(0, tiles)
+    def _(n):
+        cols = pl.ds(pl.multiple_of(n * 256, 256), 256)
+        for half in range(2):
+            wide = pl.ds(half * 512, 512)
+            total = product_left(m.hid[0, :, cols], m.cot[0, :, wide]) + product_left(m.hid[1, :, cols], m.cot[1, :, wide])
+            m.dd[cols, wide] = total.astype(BF)
+
+    pump(len(queue))
+    s_down.start()
+    tasks = s_down.steps()
+
+    def work(count):
+        for _ in range(min(count, len(tasks))):
+            tasks.pop(0)()
+
+    g_down.ready()
+    for r in range(ROWS_HERE):
+
+        @pl.loop(0, tiles)
+        def _(n, r=r):
+            first = pl.ds(pl.multiple_of(n * 256, 256), 256)
+            later = pl.ds(pl.multiple_of(HIDDEN + n * 256, 256), 256)
+            grad = product_right(m.cot[r], m.wd[first, :]).astype(BF).astype(F32)
+            m.fac[r, :, first] = (grad * m.fac[r, :, first].astype(F32)).astype(BF)
+            m.fac[r, :, later] = (grad * m.fac[r, :, later].astype(F32)).astype(BF)
+
+    second_sum.free()
+    third_sum, third_share = Reduce(m.p, m.r1, m.q2, m.r2, TOKENS), Share(m.dx2)
+    for r in range(ROWS_HERE):
+        to_owner(third_sum, lambda r, n: product_right(m.fac[r], m.wg[n * 256 : n * 256 + 256, :]), None, r)
+
+    s_gate = Scatter(lambda d: m.dg.at[pl.ds(d * SEG, SEG)], lambda b: m.xg.at[b], lambda b: m.zg.at[b], SEG)
+
+    def gate_grad(i):
+        n = i % (2 * tiles)
+        rows = pl.ds(pl.multiple_of((i // (2 * tiles)) * 256, 256), 256)
+        cols = pl.ds(pl.multiple_of(n * 256, 256), 256)
+        total = product_left(m.n2[0, :, rows], m.fac[0, :, cols]) + product_left(m.n2[1, :, rows], m.fac[1, :, cols])
+        m.dg[rows, cols] = total.astype(BF)
+
+    pl.loop(0, 4 * tiles)(gate_grad)
+    for r in range(ROWS_HERE):
+        third_sum.cross(r)
+    pl.loop(4 * tiles, 8 * tiles)(gate_grad)
+    s_gate.start()
+
+    def gradient_in(reduce, share, base, values, index, result, r):
+        reduce.arrive(r)
+        for rows in halves:
+            back = norm_back(values(r, rows), reduce.total(r, rows), index)
+            result(r, rows, (base(r, rows) + back).astype(BF))
+        if share is not None:
+            share.give(r)
+
+    def into(ref):
+        def store(r, rows, value):
+            ref[4 * r + pipe, rows] = value
+
+        return store
+
+    own_cot = lambda r, rows: m.cot[r, pl.ds(pipe * TOKENS + rows.start, TOKENS // 2)].astype(F32)
+    for r in range(ROWS_HERE):
+        gradient_in(third_sum, third_share, own_cot, own_of(m.x2), 3, into(m.dx2), r)
+
+    out_sum = Reduce(m.bp.at[:, pl.ds(0, TOKENS)], m.br1.at[:, :, pl.ds(0, TOKENS)], m.bq2.at[:, pl.ds(0, TOKENS)], m.br2.at[:, pl.ds(0, TOKENS)], TOKENS)
+    for r in range(ROWS_HERE):
+        to_owner(out_sum, lambda r, n: product(m.hid[r], m.wd[:, n * 256 : n * 256 + 256]), None, r)
+    for r in range(ROWS_HERE):
+        third_share.relay(r)
+    for r in range(ROWS_HERE):
+        out_sum.cross(r)
+
+    def rows_of(ref, r):
+        return ref[4 * r : 4 * r + 4].reshape(PATCHES, WIDTH)
+
+    def mixed_back(share, grads, layer, r):
+        share.ready(r)
+        m.dmix[r] = product_right(rows_of(grads, r), m.woh[layer].reshape(MINE, WIDTH)).astype(BF)
+
+    for r in range(ROWS_HERE):
+        mixed_back(third_share, m.dx2, 1, r)
+
+    @pl.loop(0, ROWS_HERE)
+    def _(r):
+        attend_back(r, causal(r), queries, keys, values, m.dmix, m.dqkv.at[0], m.dqkv.at[1], m.dqkv.at[2])
+
+    third_sum.free()
+    fourth_sum, fourth_share = Reduce(m.p, m.r1, m.q2, m.r2, TOKENS), Share(m.dx1)
+
+    def attn_back(r, n, layer, parts):
+        rows = pl.ds(n * 256, 256)
+        total = None
+        for part, ref in parts:
+            term = product_right(ref[r], m.wa[3 * layer + part, rows, :])
+            total = term if total is None else total + term
+        return total
+
+    for r in range(ROWS_HERE):
+        to_owner(fourth_sum, lambda r, n: attn_back(r, n, 1, [(i, m.dqkv.at[i]) for i in range(3)]), None, r)
+
+    def own_half(layer, which):
+        return m.won.at[layer, :, which]
+
+    def out_grad(layer, mixed, grads):
+        (g_out0, g_out1)[layer].finish()
+        (swap0, swap1)[layer][1].wait_send()
+        for n in range(4):
+            cols = pl.ds(n * 256, 256)
+            total = None
+            for r in range(ROWS_HERE):
+                term = product_left(mixed[r], grads[4 * r : 4 * r + 4, :, cols].reshape(PATCHES, 256))
+                total = term if total is None else total + term
+            m.won[layer, :, :, :, cols] = total.astype(BF).reshape(LINE, SIDE, SHARD, 256)
+        there = m.don.at[layer, pl.ds(HEADS_MINE * c, HEADS_MINE)]
+        keep = near(own_half(layer, c), there)
+        give = remote(own_half(layer, 1 - c), there, sibling)
+        begin(give)
+        return keep, give
+
+    def attn_grad(layer, part, left, right, count):
+        @pl.loop(0, 4)
+        def _(n):
+            cols = pl.ds(pl.multiple_of(n * 256, 256), 256)
+            total = None
+            for r in range(ROWS_HERE):
+                term = product_left(left[r, :, cols], right[r])
+                total = term if total is None else total + term
+            m.da[3 * layer + part, cols, :] = total.astype(BF)
+
+    def scatter_out(layer):
+        return Scatter(lambda d: m.don.at[layer, d], lambda b: m.xo.at[layer, b], lambda b: m.zo.at[layer, b], SHARD)
+
+    def scatter_attn(first, count):
+        part = pl.ds(first, count)
+        return Scatter(
+            lambda d: m.da.at[part, pl.ds(d * SEG, SEG)], lambda b: m.xa.at[part, b], lambda b: m.za.at[part, b], SEG
+        )
+
+    swap2 = out_grad(1, m.o, m.dx2)
+    for r in range(ROWS_HERE):
+        fourth_sum.cross(r)
+    for part in range(3):
+        attn_grad(1, part, m.n1, m.dqkv.at[part], PATCHES)
+    s_attn1, s_out1 = scatter_attn(3, 3), scatter_out(1)
+    s_attn1.start()
+    swap2[0].wait()
+    swap2[1].wait_recv()
+    s_out1.start()
+    for r in range(ROWS_HERE):
+        out_sum.arrive(r)
+        for rows in halves:
+            m.out[r, rows] = (own_of(m.x2)(r, rows) + out_sum.total(r, rows)).astype(BF)
+    for r in range(ROWS_HERE):
+        gradient_in(fourth_sum, fourth_share, own_of(m.dx2), own_of(m.x1), 2, into(m.dx1), r)
+    for r in range(ROWS_HERE):
+        fourth_share.relay(r)
+    work(2)
+    for r in range(ROWS_HERE):
+        mixed_back(fourth_share, m.dx1, 0, r)
+
+    @pl.loop(0, ROWS_HERE)
+    def _(r):
+        attend_back(r, window(r), m.qc, m.kc, m.vc, m.dmix, m.dqc, m.dkc, m.dvc)
+
+    out_sum.free()
+    fourth_sum.free()
+    byte_sum = Reduce(m.bp, m.br1, m.bq2, m.br2, TOKENS_B)
+    fifth_sum = Reduce(m.p, m.r1, m.q2, m.r2, TOKENS)
+    for r in range(ROWS_HERE):
+        to_owner(
+            byte_sum,
+            lambda r, n: product_right(m.dkc[r], m.wa[1, n * 256 : n * 256 + 256, :])
+            + product_right(m.dvc[r], m.wa[2, n * 256 : n * 256 + 256, :]),
+            None,
+            r,
+        )
+    for r in range(ROWS_HERE):
+        to_owner(fifth_sum, lambda r, n: product_right(m.dqc[r], m.wa[0, n * 256 : n * 256 + 256, :]), None, r)
+    own_bytes = [near(m.byte.at[4 * r + pipe], m.bown.at[r]) for r in range(ROWS_HERE)]
+    swap3 = out_grad(0, m.oc, m.dx1)
+    for r in range(ROWS_HERE):
+        byte_sum.cross(r)
+    attn_grad(0, 1, m.nb, m.dkc, BYTES)
+    attn_grad(0, 2, m.nb, m.dvc, BYTES)
+    attn_grad(0, 0, m.nq, m.dqc, PATCHES)
+    s_attn0, s_out0 = scatter_attn(0, 3), scatter_out(0)
+    s_attn0.start()
+    swap3[0].wait()
+    swap3[1].wait_recv()
+    s_out0.start()
+    for r in range(ROWS_HERE):
+        fifth_sum.cross(r)
+
+    def back_to_pipe(rows_ref, dst):
+        copies = [near(rows_ref(pipe), dst)]
+        for device in (across, corner, sibling):
+            copies.append(begin(remote(rows_ref(device[1]), dst, device)))
+        return copies
+
+    def attn_home(layer):
+        src = lambda q: m.da.at[pl.ds(3 * layer, 3), pl.ds(dp * SEG + q * SHARD, SHARD)]
+        return back_to_pipe(src, m.g_attn.at[pipe, pl.ds(3 * layer, 3)])
+
+    def gate_home():
+        src = lambda q: m.dg.at[pl.ds(dp * SEG + q * SHARD, SHARD)]
+        return back_to_pipe(src, m.g_gate.at[pipe])
+
+    work(len(tasks))
+    tasks += s_gate.steps()
+    work(len(tasks))
+    home = [gate_home()]
+    for r in range(ROWS_HERE):
+        gradient_in(
+            fifth_sum,
+            None,
+            own_of(m.dx1),
+            own_patch,
+            0,
+            lambda r, rows, value: m.gpatch.__setitem__((r, rows), value),
+            r,
+        )
+    for copy in own_bytes:
+        copy.wait()
+    for r in range(ROWS_HERE):
+        byte_sum.arrive(r)
+        for part in range(5):
+            rows = pl.ds(part * 32, 32)
+            back = norm_back(m.bown[r, rows], byte_sum.total(r, rows), 1)
+            m.gbyte[r, rows] = back.astype(BF)
+
+    gain_steps = []
+    for k, device in enumerate((sibling, across, aside, pair, mirror)):
+
+        def gain_step(k=k, device=device):
+            m.gs[k] = m.gn[...]
+            copy = begin(remote(m.gs.at[k], m.gr.at[k], device))
+
+            def done():
+                copy.wait_recv()
+                m.gn[...] += m.gr[k]
+
+            return done
+
+        gain_steps.append(gain_step)
+
+    tasks += s_attn1.steps()
+    work(len(tasks))
+    home.append(attn_home(1))
+    tasks += s_out1.steps()
+    pending = gain_steps[0]()
+    work(3)
+    pending()
+    pending = gain_steps[1]()
+    work(len(tasks))
+    pending()
+    pending = gain_steps[2]()
+    tasks += s_attn0.steps()
+    work(3)
+    pending()
+    pending = gain_steps[3]()
+    work(len(tasks))
+    home.append(attn_home(0))
+    pending()
+    pending = gain_steps[4]()
+    tasks += s_out0.steps()
+    work(len(tasks))
+    pending()
+    m.g_gain[...] = m.gn[...]
+    m.g_down[...] = m.dd[pl.ds(dp * PADDED, PADDED), :]
+    for layer in range(2):
+        m.g_out[layer] = m.don[layer, dp]
+    for copies in home:
+        arrived(copies)
+    for gather in (g_attn0, g_attn1, g_gate, g_down):
+        gather.finish()
+    for scatter in (s_down, s_gate, s_attn1, s_out1, s_attn0, s_out0):
+        scatter.finish()
+    byte_sum.free()
+    fifth_sum.free()
+    for wait in unfinished:
+        wait()
+
+
+def fused_step(patch_states, byte_states, cotangent, patch_lengths, row_lengths, attn_weights, out_weights, gate_up, down_weight, gains):
+    wa = attn_weights.reshape(6, SHARD, 2, HEADS_MINE, 2, HEAD_DIM).transpose(4, 2, 0, 1, 3, 5).reshape(RANKS, 6, SHARD, MINE)
+    wg = gate_up.reshape(2, SHARD, GROUPS, RANKS, UNITS)
+    wg = jnp.pad(wg, ((0, 0),) * 4 + ((0, PADDED - UNITS),)).transpose(3, 1, 0, 2, 4).reshape(RANKS, SHARD, 2 * HIDDEN)
+    wd = jnp.pad(down_weight, ((0, PADDED - UNITS), (0, 0)))
+    lens = jnp.concatenate(
+        [patch_lengths.astype(F32), jnp.broadcast_to(row_lengths.astype(F32)[:, None], (ROWS_HERE, PATCHES))], axis=0
+    )
+    lens = jnp.pad(lens, ((0, 4), (0, 0)))
+    gains = jnp.pad(gains, ((0, 4), (0, 0)))
+    plan = scratch_plan()
+    vmem, anywhere = pl.BlockSpec(memory_space=pltpu.VMEM), pl.BlockSpec(memory_space=pl.ANY)
+    shape = jax.ShapeDtypeStruct
+    results = pl.pallas_call(
+        functools.partial(step_kernel, tuple(plan)),
+        out_shape=(
+            shape((ROWS_HERE, TOKENS, WIDTH), BF),
+            shape((ROWS_HERE, TOKENS, WIDTH), BF),
+            shape((ROWS_HERE, TOKENS_B, WIDTH), BF),
+            shape((RANKS, 6, SHARD, MINE), BF),
+            shape((2, SHARD, WIDTH), BF),
+            shape((RANKS, SHARD, 2 * HIDDEN), BF),
+            shape((PADDED, WIDTH), BF),
+            shape((8, WIDTH), F32),
+        ),
+        in_specs=[vmem, anywhere, vmem, vmem, vmem, anywhere, anywhere, anywhere, anywhere],
+        out_specs=[vmem] * 8,
+        scratch_shapes=list(plan.values()),
+        compiler_params=pltpu.CompilerParams(collective_id=0, has_side_effects=True, vmem_limit_bytes=63 * 2**20),
+    )(patch_states, byte_states.reshape(8, TOKENS_B, WIDTH), cotangent, lens, gains, wa, wg, out_weights, wd)
+    out, gpatch, gbyte, g_attn, g_out, g_gate, g_down, g_gain = results
+    g_attn = g_attn.reshape(2, 2, 6, SHARD, HEADS_MINE, HEAD_DIM).transpose(2, 3, 1, 4, 0, 5)
+    g_attn = g_attn.reshape(2, 3, SHARD, WIDTH).astype(F32)
+    g_gate = g_gate.reshape(RANKS, SHARD, 2, GROUPS, PADDED)[..., :UNITS].transpose(2, 1, 3, 0, 4)
+    g_gate = g_gate.reshape(2, SHARD, GROUPS * RANKS * UNITS).astype(F32)
+    first = (lax.axis_index("dp") * RANKS + lax.axis_index("pipe")) * SHARD
+    g_gain = lax.dynamic_slice(g_gain, (0, first), (4, SHARD))
+    return out, gpatch, gbyte, g_attn, g_out.astype(F32), g_gate, g_down[:UNITS].astype(F32), g_gain
+
+
 def solution(mesh):
     placed = (
         P("dp", None, None),
@@ -189,7 +1099,7 @@
         P(),
     )
     return jax.shard_map(
-        local,
+        fused_step if mesh.shape["dp"] == GROUPS else gathered_step,
         mesh=mesh,
         in_specs=placed,
         out_specs=(

time: 1210 us -> 476 us (0.39)
  the two profiles are of different devices: /device:TPU:0 before, /device:TPU:14 now
where the time goes in v2:
time: 476 us; the launch traced here: 470 us
  Pallas kernels  446 us (94%)
  local copies, waits for them, and re-layouts  20.8 us (4%)
    pallas_call x1, Pallas kernels, fused_step(): pl.pallas_call(functools.partial(step_kernel, tuple(plan)), out_shape=(sh...  446 us

profile of v2, /device:TPU:14, one launch (start us, length us, event | category | flops | bytes accessed | tf_op | source)
XLA Modules:
  0.0 469.7 jit_solution(12997886069800650763)
XLA Ops:
  0.6 2.3 reshape.45
  3.0 0.3 copy.23
  3.3 1.2 reshape.46.refs_5_
  4.6 1.3 reshape.47
  6.0 0.1 pad_bitcast_fusion
  6.1 1.3 reshape.48.refs_6_
  7.4 0.7 pad.19.refs_8_
  8.1 0.6 pad.17.refs_4_
  8.7 0.1 pad.21.clone
  8.9 0.6 pad.16.refs_3_
  9.5 446.0 %shard_map.161 = (bf16[2,64,1024]{2,1,0:T(8,128)(2,1)}, bf16[2,64,1024]{2,1,0:T(8,128)(2,1)}, bf16[2,160,1024]{2,1,0:T(8,128)(2,1)}, bf16[4,6,32,256]{3,2,1,0:T(...) custom-call(bf16[2,256,1024]{2,1,0:T(8,128)(2,1)} %refs_0_.1, ...), custom_call_target="tpu_custom_call" | custom-call | tf_op jit(solution)/shard_map/pallas_call | solution.py:1061
  455.5 1.3 constant_dynamic-slice_fusion
  456.8 1.8 reshape.52
  458.7 1.2 copy.20
  459.9 2.3 reshape.50
  462.3 0.5 reshape.49
  462.7 0.1 convert_bitcast_fusion
  462.8 0.7 copy.21
  463.5 2.0 reshape.51
  465.5 0.8 slice_convert_fusion
  466.3 0.7 convert_element_type.47
  467.0 0.7 copy.27
  467.7 0.7 copy.28
  468.4 0.8 copy.29
  (26 shorter events, 0.2 us)
Async XLA Ops:
  3.0 1.6 copy-start.2
  5.8 1.6 copy-start.5
  5.9 2.2 copy-start.8
  5.9 2.8 copy-start.9
  5.9 2.8 copy-start.10
  459.9 2.4 copy-start.1
  462.8 2.7 copy-start.6
  463.5 2.8 copy-start.7
  463.5 3.5 copy-start.4
  463.5 4.2 copy-start.3
  463.5 4.9 %copy-start = (bf16[2,160,1024]{2,1,0:T(8,128)(2,1)S(1)}, bf16[2,160,1024]{2,1,0:T(8,128)(2,1)}, u32[]{:S(2)}) copy-start(bf16[2,160,1024]{2,1,0:T(8,128)(2,1)} %get-tuple-element.34) | copy-start | bytes 1966084
